TPU v7x, 512 devices: a whole 4x4x16 slice. The times are simulated.
512 devices in a mesh: sector: 128 (over z, x, y_lo), slab: 4 (over y_hi, core).
Axes of the slice: x: 4, y: 4 (y_hi: 2, y_lo: 2; y = y_hi * 2 + y_lo), z: 16, core: 2. Of those that a mesh axis runs over, the one named last changes fastest.
Arguments:
- state: float32 [5, 64, 1024, 128], P(None, 'slab', 'sector'), may hold values from -6 to 6
- mean_velocity: float32 [64, 1024, 128], P('slab', 'sector'), may hold values from 0.2 to 1.2
- sound_speed: float32 [64, 1024, 128], P('slab', 'sector'), may hold values from 0.5 to 2
- flux_axial: float32 [5, 5], replicated, may hold values from -2 to 2
- flux_radial: float32 [5, 5], replicated, may hold values from -2 to 2
- flux_azimuthal: float32 [5, 5], replicated, may hold values from -2 to 2
- axis_pair: int32 [128, 8], P('sector'), may hold values from 0 to 7, each once within a row
- panel_weight: float32 [4, 49152], P('slab', 'sector'), may hold values from 0.25 to 1.75
- panel_cell: int32 [4, 49152], P('slab', 'sector'), may hold values from 0 to 127
- panel_owner: int32 [4, 49152, 1], P('slab', 'sector'), may hold values from 0 to 127; in each aligned block of 384 rows (0 to 383, 384 to 767, ..., all dimensions but the last counted through in order) at most 4 rows name the same one
- panel_count: int32 [4, 128], P('slab', 'sector'), may hold values from 1 to 384, 16384 in all within a row
Outputs:
- sensitivity: float32 [5, 64, 1024, 128], P(None, 'slab', 'sector')
- harmonics: float32 [4, 128, 31, 128], P('slab', 'sector')
Inputs may be any that keep to these rules, and one draw needn't show every extreme that they name: `panel_owner`: in each device's 384 slots no owner is named more than 4 times, and some device names one owner exactly 4 times. `panel_count`: live slots of the device; some device has all 384 live. `axis_pair`: each row is a permutation of the columns.
All inputs are finite; a program needn't handle non-finite values.
Results may differ from a plain program's by a relative error of at most 0.0003.
Values sent between devices are 32-bit elements; how exact they have to be, the bound alone decides.
A program may use at most 64 MiB of HBM per device.

v0:
```python
import math

import jax
import jax.numpy as jnp
from jax import lax
from jax.sharding import PartitionSpec as P

PLANES = 16
COLS = 8
RADII = 128
PANELS = 384
ORDERS = 16
MODES = 31


PRECISE = lax.Precision.HIGHEST
PARITY_SIGNS = (1.0, 1.0, -1.0, -1.0, 1.0)
TIME_STEP = 0.25
VISCOSITY = 0.05


def with_halo(shard, sides, width, wrap):
    for axis, dim in sides:
        size, length = (lax.axis_size(axis), shard.shape[dim])
        up = [(i, (i + 1) % size) for i in range(size if wrap else size - 1)]
        down = [(j, i) for i, j in up]
        last = lax.slice_in_dim(shard, length - width, length, axis=dim)
        initial = lax.slice_in_dim(shard, 0, width, axis=dim)
        before = lax.ppermute(last, axis, up)
        after = lax.ppermute(initial, axis, down)
        shard = jnp.concatenate([before, shard, after], axis=dim)
    return shard


def from_behind(shard, axis, by):
    length = lax.axis_size(axis)
    return lax.ppermute(shard, axis, [(i, (i + by) % length) for i in range(length)])


def neighbours(field, pair_pick, signs):
    fields, planes, columns, radial = field.shape
    beside_all = with_halo(field, (("sector", 2),), 1, True)
    axial_pad = with_halo(field, (("slab", 1),), 1, False)
    inner_row = field[..., 0].reshape(fields, planes * columns)
    sectors = lax.axis_size("sector")
    facing = from_behind(inner_row, "sector", sectors // 2)
    facing = facing.reshape(fields, planes, columns)
    mirror = jnp.einsum("fic,dc->fid", facing, pair_pick, precision=PRECISE) * signs[:, None, None]
    zero_cycle = jnp.zeros_like(field[..., :1])
    r_minus = jnp.concatenate([mirror[..., None], field[..., :-1]], 3)
    r_plus = jnp.concatenate([field[..., 1:], zero_cycle], 3)
    return (
        axial_pad[:, :-2],
        axial_pad[:, 2:],
        beside_all[:, :, :-2],
        beside_all[:, :, 2:],
        r_minus,
        r_plus,
    )


def couple(matrix, field):
    return jnp.einsum("fg,g...->f...", matrix, field, precision=PRECISE)


def laplace(field, near):
    return near[0] + near[1] + near[2] + near[3] + near[4] + near[5] - 6.0 * field


def forward_rate(field, near, coefs, fluxes, inverse_radius):
    axial_diff = 0.5 * (near[1] - near[0])
    angle_diff = 0.5 * (near[3] - near[2])
    radial_diff = 0.5 * (near[5] - near[4])
    mixed = (
        couple(fluxes[0], axial_diff)
        + couple(fluxes[1], radial_diff)
        + inverse_radius * couple(fluxes[2], angle_diff)
    )
    return -coefs[0] * axial_diff - coefs[1] * mixed + VISCOSITY * laplace(field, near)


def adjoint_rate(field, near, coef_near, fluxes, inverse_radius):
    carried = 0.5 * (coef_near[1][0] * near[1] - coef_near[0][0] * near[0])
    axial_diff = 0.5 * (coef_near[1][1] * near[1] - coef_near[0][1] * near[0])
    angle_diff = 0.5 * (coef_near[3][1] * near[3] - coef_near[2][1] * near[2])
    radial_diff = 0.5 * (coef_near[5][1] * near[5] - coef_near[4][1] * near[4])
    mixed = (
        couple(fluxes[0].T, axial_diff)
        + couple(fluxes[1].T, radial_diff)
        + inverse_radius * couple(fluxes[2].T, angle_diff)
    )
    return carried + mixed + VISCOSITY * laplace(field, near)


def basis_rows(angle):
    orders = jnp.arange(ORDERS, dtype=jnp.float32)
    cosines = jnp.cos(angle[..., None] * orders)
    sines = jnp.sin(angle[..., None] * orders[1:])
    return jnp.concatenate([cosines, sines], -1)


def local(
    state,
    mean_velocity,
    sound_speed,
    flux_axial,
    flux_radial,
    flux_azimuthal,
    axis_pair,
    panel_weight,
    panel_cell,
    panel_owner,
    panel_count,
):
    sectors = lax.axis_size("sector")
    sector = lax.axis_index("sector")
    azimuth = COLS * sectors
    capacity = max(4, 3 * PANELS // (2 * sectors))
    pair_pick = (axis_pair[0][:, None] == jnp.arange(COLS, dtype=jnp.int32)[None, :]).astype(
        jnp.float32
    )
    signs = jnp.array(PARITY_SIGNS, jnp.float32)
    coefs = jnp.stack([mean_velocity, sound_speed])
    coef_near = neighbours(coefs, pair_pick, jnp.ones((2,), jnp.float32))
    inverse_radius = 1.0 / (jnp.arange(RADII, dtype=jnp.float32) + 0.5)
    fluxes = (flux_axial, flux_radial, flux_azimuthal)
    current = state
    for section in range(2):
        near = neighbours(current, pair_pick, signs)
        current = current + TIME_STEP * forward_rate(current, near, coefs, fluxes, inverse_radius)
    forward = current
    encode_scale = PANELS ** (-0.5)
    pressure = forward[4].reshape(PLANES * COLS, RADII)
    cells = panel_cell[0]
    owner = panel_owner[0, :, 0]
    alive = (jnp.arange(PANELS, dtype=jnp.int32) < panel_count[0, 0]).astype(jnp.float32)
    factor = panel_weight[0] * alive
    cell_pick = (cells[:, None] == jnp.arange(PLANES * COLS, dtype=jnp.int32)[None, :]).astype(
        jnp.float32
    )
    lines = jnp.dot(cell_pick, pressure, precision=PRECISE) * factor[:, None]
    column = sector * COLS + cells % COLS
    angle = column.astype(jnp.float32) * (2.0 * math.pi / azimuth)
    owner_pick = (owner[:, None] == jnp.arange(sectors, dtype=jnp.int32)[None, :]).astype(
        jnp.float32
    )
    earlier = jnp.cumsum(owner_pick, 0) - owner_pick
    slot_index = owner * capacity + jnp.sum(earlier * owner_pick, 1).astype(jnp.int32)
    slot_pick = (
        slot_index[:, None] == jnp.arange(sectors * capacity, dtype=jnp.int32)[None, :]
    ).astype(jnp.float32)
    outgoing = jnp.dot(slot_pick.T, lines, precision=PRECISE).reshape(sectors, capacity, RADII)
    out_angle = jnp.dot(slot_pick.T, angle[:, None], precision=PRECISE).reshape(sectors, capacity)
    incoming, in_angle = (
        lax.all_to_all(outgoing, "sector", split_axis=0, concat_axis=0, tiled=True),
        lax.all_to_all(out_angle, "sector", split_axis=0, concat_axis=0, tiled=True),
    )
    received_phase = basis_rows(in_angle.reshape(sectors * capacity))
    harmonics = encode_scale * jnp.dot(
        received_phase.T, incoming.reshape(sectors * capacity, RADII), precision=PRECISE
    )
    reply = encode_scale * jnp.dot(received_phase, harmonics, precision=PRECISE)
    returned = lax.all_to_all(
        reply.reshape(sectors, capacity, RADII), "sector", split_axis=0, concat_axis=0, tiled=True
    )
    gradient = jnp.dot(slot_pick, returned.reshape(sectors * capacity, RADII), precision=PRECISE)
    impulse = jnp.dot(cell_pick.T, gradient * factor[:, None], precision=PRECISE).reshape(
        PLANES, COLS, RADII
    )
    current = forward.at[4].add(impulse)
    for section in range(2):
        near = neighbours(current, pair_pick, signs)
        current = current + TIME_STEP * adjoint_rate(
            current, near, coef_near, fluxes, inverse_radius
        )
    return (current, harmonics.reshape(1, 1, MODES, RADII))


def solution(mesh):
    return jax.shard_map(
        local,
        mesh=mesh,
        in_specs=(
            P(None, "slab", "sector", None),
            P("slab", "sector", None),
            P("slab", "sector", None),
            P(),
            P(),
            P(),
            P("sector", None),
            P("slab", "sector"),
            P("slab", "sector"),
            P("slab", "sector", None),
            P("slab", "sector"),
        ),
        out_specs=(P(None, "slab", "sector", None), P("slab", "sector", None, None)),
        check_vma=False,
    )
```

profile of v0, /device:TPU:1, one launch (start us, length us, event | category | flops | bytes accessed | tf_op | source)
XLA Modules:
  0.0 220.4 jit_solution(14205165233605006859)
XLA Ops:
  1.9 8.9 %collective-permute-start = (f32[5,1,8,128]{3,0,2,1:T(8,128)S(1)}, f32[5,1,8,128]{3,0,2,1:T(8,128)S(1)}, u32[]{:S(2)}, u32[]{:S(2)}) collective-permute-start(f32[5,1,8,128]{3,0,2,1:T(8,128)S(1)} %get-tuple-element.47), channel_id=1, source_target_pairs={{1,0},{2,1},{3,2},{5,4},{6,5},{7,6},{9,8},{10,9},{11,10},{13,12},{... | collective-permute-start | bytes 61448 | tf_op jit(solution)/shard_map/ppermute | solution.py:30
  12.7 11.5 %collective-permute-start.3 = (f32[5,16,1,128]{3,0,2,1:T(8,128)S(1)}, f32[5,16,1,128]{3,0,2,1:T(8,128)S(1)}, u32[]{:S(2)}, u32[]{:S(2)}) collective-permute-start(f32[5,16,1,128]{3,0,2,1:T(8,128)S(1)} %get-tuple-element.43), channel_id=1, source_target_pairs={{4,0},{8,4},{12,8},{16,12},{20,16},{24,20},{28,24},{32,28},{36,32}... | collective-permute-start | bytes 122888 | tf_op jit(solution)/shard_map/ppermute | solution.py:30
  24.5 6.1 %collective-permute-start.2 = (f32[5,128]{1,0:T(8,128)S(1)}, f32[5,128]{1,0:T(8,128)S(1)}, u32[]{:S(2)}, u32[]{:S(2)}) collective-permute-start(f32[5,128]{1,0:T(8,128)S(1)} %reshape_squeeze.18), channel_id=1, source_target_pairs={{0,256},{4,260},{8,264},{12,268},{16,272},{20,276},{24,280},{28,28... | collective-permute-start | bytes 7688 | tf_op jit(solution)/shard_map/ppermute | solution.py:37
  36.1 12.8 %all-to-all-start = ((f32[128,1,4]{2,1,0:T(1,128)}), f32[128,1,4]{2,1,0:T(1,128)S(1)}, u32[]{:S(2)}, u32[]{:S(2)}) async-start(f32[128,1,4]{2,1,0:T(1,128)} %bitcast.20), calls=%async_computation | async-start | bytes 131072 | tf_op jit(solution)/shard_map/all_to_all | solution.py:156
  55.8 11.5 %collective-permute-start.7 = (f32[5,128]{1,0:T(8,128)S(1)}, f32[5,128]{1,0:T(8,128)S(1)}, u32[]{:S(2)}, u32[]{:S(2)}) collective-permute-start(f32[5,128]{1,0:T(8,128)S(1)} %reshape_squeeze.19), channel_id=1, source_target_pairs={{0,256},{4,260},{8,264},{12,268},{16,272},{20,276},{24,280},{28,28... | collective-permute-start | bytes 7688 | tf_op jit(solution)/shard_map/ppermute | solution.py:37
  69.3 5.1 %collective-permute-start.6 = (f32[5,1,8,128]{3,0,2,1:T(8,128)S(1)}, f32[5,1,8,128]{3,0,2,1:T(8,128)S(1)}, u32[]{:S(2)}, u32[]{:S(2)}) collective-permute-start(f32[5,1,8,128]{3,0,2,1:T(8,128)S(1)} %get-tuple-element.40), channel_id=1, source_target_pairs={{0,1},{1,2},{2,3},{4,5},{5,6},{6,7},{8,9},{9,10},{10,11},{12,13},{... | collective-permute-start | bytes 61448 | tf_op jit(solution)/shard_map/ppermute | solution.py:29
  74.4 5.2 %collective-permute-start.8 = (f32[5,16,1,128]{3,0,2,1:T(8,128)S(1)}, f32[5,16,1,128]{3,0,2,1:T(8,128)S(1)}, u32[]{:S(2)}, u32[]{:S(2)}) collective-permute-start(f32[5,16,1,128]{3,0,2,1:T(8,128)S(1)} %get-tuple-element.37), channel_id=1, source_target_pairs={{4,0},{8,4},{12,8},{16,12},{20,16},{24,20},{28,24},{32,28},{36,32}... | collective-permute-start | bytes 122888 | tf_op jit(solution)/shard_map/ppermute | solution.py:30
  83.9 4.9 %collective-permute-done.9 = f32[5,16,1,128]{3,0,2,1:T(8,128)S(1)} collective-permute-done((f32[5,16,1,128]{3,0,2,1:T(8,128)S(1)}, f32[5,16,1,128]{3,0,2,1:T(8,128)S(1)}, u32[]{:S(2)}, u32[]{:S(2)}) %collective-permute-start.9) | collective-permute-done | bytes 40992 | tf_op jit(solution)/shard_map/ppermute | solution.py:29
  92.0 6.5 %all-to-all-start.1 = ((f32[128,4,128]{2,1,0:T(4,128)}), f32[128,4,128]{2,1,0:T(4,128)S(1)}, u32[]{:S(2)}, u32[]{:S(2)}) async-start(f32[128,4,128]{2,1,0:T(4,128)} %bitcast.23), calls=%async_computation.1 | async-start | bytes 524288 | tf_op jit(solution)/shard_map/all_to_all | solution.py:155
  100.3 17.6 %all-to-all-done.1 = f32[128,4,128]{2,1,0:T(4,128)S(1)} async-done(((f32[128,4,128]{2,1,0:T(4,128)}), f32[128,4,128]{2,1,0:T(4,128)S(1)}, u32[]{:S(2)}, u32[]{:S(2)}) %all-to-all-start.1) | async-done | bytes 262176 | tf_op jit(solution)/shard_map/all_to_all | solution.py:155
  119.5 8.9 %all-to-all-start.2 = ((f32[128,4,128]{2,1,0:T(4,128)}), f32[128,4,128]{2,1,0:T(4,128)S(1)}, u32[]{:S(2)}, u32[]{:S(2)}) async-start(f32[128,4,128]{2,1,0:T(4,128)} %bitcast.25), calls=%async_computation.2 | async-start | bytes 524288 | tf_op jit(solution)/shard_map/all_to_all | solution.py:163
  128.4 2.6 %collective-permute-start.10 = (f32[2,1,8,128]{3,2,1,0:T(8,128)S(1)}, f32[2,1,8,128]{3,2,1,0:T(8,128)S(1)}, u32[]{:S(2)}, u32[]{:S(2)}) collective-permute-start(f32[2,1,8,128]{3,2,1,0:T(8,128)S(1)} %get-tuple-element.60), channel_id=1, source_target_pairs={{1,0},{2,1},{3,2},{5,4},{6,5},{7,6},{9,8},{10,9},{11,10},{13,12},{... | collective-permute-start | bytes 24584 | tf_op jit(solution)/shard_map/ppermute | solution.py:30
  131.0 4.5 %collective-permute-start.12 = (f32[2,1,8,128]{3,2,1,0:T(8,128)S(1)}, f32[2,1,8,128]{3,2,1,0:T(8,128)S(1)}, u32[]{:S(2)}, u32[]{:S(2)}) collective-permute-start(f32[2,1,8,128]{3,2,1,0:T(8,128)S(1)} %get-tuple-element.61), channel_id=1, source_target_pairs={{0,1},{1,2},{2,3},{4,5},{5,6},{6,7},{8,9},{9,10},{10,11},{12,13},{... | collective-permute-start | bytes 24584 | tf_op jit(solution)/shard_map/ppermute | solution.py:29
  135.5 2.5 %collective-permute-start.18 = (f32[2,16,1,128]{3,2,1,0:T(1,128)S(1)}, f32[2,16,1,128]{3,2,1,0:T(1,128)S(1)}, u32[]{:S(2)}, u32[]{:S(2)}) collective-permute-start(f32[2,16,1,128]{3,2,1,0:T(1,128)S(1)} %get-tuple-element.57), channel_id=1, source_target_pairs={{0,4},{4,8},{8,12},{12,16},{16,20},{20,24},{24,28},{28,32},{32,36}... | collective-permute-start | bytes 49160 | tf_op jit(solution)/shard_map/ppermute | solution.py:29
  138.0 7.0 %collective-permute-start.16 = (f32[2,16,1,128]{3,2,1,0:T(1,128)S(1)}, f32[2,16,1,128]{3,2,1,0:T(1,128)S(1)}, u32[]{:S(2)}, u32[]{:S(2)}) collective-permute-start(f32[2,16,1,128]{3,2,1,0:T(1,128)S(1)} %get-tuple-element.56), channel_id=1, source_target_pairs={{4,0},{8,4},{12,8},{16,12},{20,16},{24,20},{28,24},{32,28},{36,32}... | collective-permute-start | bytes 49160 | tf_op jit(solution)/shard_map/ppermute | solution.py:30
  145.2 11.5 %collective-permute-start.14 = (f32[2,128]{1,0:T(2,128)S(1)}, f32[2,128]{1,0:T(2,128)S(1)}, u32[]{:S(2)}, u32[]{:S(2)}) collective-permute-start(f32[2,128]{1,0:T(2,128)S(1)} %reshape_squeeze.21), channel_id=1, source_target_pairs={{0,256},{4,260},{8,264},{12,268},{16,272},{20,276},{24,280},{28,28... | collective-permute-start | bytes 3080 | tf_op jit(solution)/shard_map/ppermute | solution.py:37
  162.8 11.5 %collective-permute-start.15 = (f32[5,128]{1,0:T(8,128)S(1)}, f32[5,128]{1,0:T(8,128)S(1)}, u32[]{:S(2)}, u32[]{:S(2)}) collective-permute-start(f32[5,128]{1,0:T(8,128)S(1)} %reshape_squeeze.22), channel_id=1, source_target_pairs={{0,256},{4,260},{8,264},{12,268},{16,272},{20,276},{24,280},{28,28... | collective-permute-start | bytes 7688 | tf_op jit(solution)/shard_map/ppermute | solution.py:37
  174.3 3.9 %collective-permute-start.13 = (f32[5,1,8,128]{3,0,2,1:T(8,128)S(1)}, f32[5,1,8,128]{3,0,2,1:T(8,128)S(1)}, u32[]{:S(2)}, u32[]{:S(2)}) collective-permute-start(f32[5,1,8,128]{3,0,2,1:T(8,128)S(1)} %get-tuple-element.35), channel_id=1, source_target_pairs={{0,1},{1,2},{2,3},{4,5},{5,6},{6,7},{8,9},{9,10},{10,11},{12,13},{... | collective-permute-start | bytes 61448 | tf_op jit(solution)/shard_map/ppermute | solution.py:29
  182.1 3.4 %collective-permute-start.19 = (f32[5,16,1,128]{3,0,2,1:T(8,128)S(1)}, f32[5,16,1,128]{3,0,2,1:T(8,128)S(1)}, u32[]{:S(2)}, u32[]{:S(2)}) collective-permute-start(f32[5,16,1,128]{3,0,2,1:T(8,128)S(1)} %get-tuple-element.30), channel_id=1, source_target_pairs={{0,4},{4,8},{8,12},{12,16},{16,20},{20,24},{24,28},{28,32},{32,36}... | collective-permute-start | bytes 122888 | tf_op jit(solution)/shard_map/ppermute | solution.py:29
  188.0 3.4 %collective-permute-done.19 = f32[5,16,1,128]{3,0,2,1:T(8,128)S(1)} collective-permute-done((f32[5,16,1,128]{3,0,2,1:T(8,128)S(1)}, f32[5,16,1,128]{3,0,2,1:T(8,128)S(1)}, u32[]{:S(2)}, u32[]{:S(2)}) %collective-permute-start.19) | collective-permute-done | bytes 40992 | tf_op jit(solution)/shard_map/ppermute | solution.py:29
  194.1 3.8 %collective-permute-start.22 = (f32[5,128]{1,0:T(8,128)S(1)}, f32[5,128]{1,0:T(8,128)S(1)}, u32[]{:S(2)}, u32[]{:S(2)}) collective-permute-start(f32[5,128]{1,0:T(8,128)S(1)} %reshape_squeeze.23), channel_id=1, source_target_pairs={{0,256},{4,260},{8,264},{12,268},{16,272},{20,276},{24,280},{28,28... | collective-permute-start | bytes 7688 | tf_op jit(solution)/shard_map/ppermute | solution.py:37
  197.9 7.5 %collective-permute-start.21 = (f32[5,1,8,128]{3,0,2,1:T(8,128)S(1)}, f32[5,1,8,128]{3,0,2,1:T(8,128)S(1)}, u32[]{:S(2)}, u32[]{:S(2)}) collective-permute-start(f32[5,1,8,128]{3,0,2,1:T(8,128)S(1)} %get-tuple-element.29), channel_id=1, source_target_pairs={{0,1},{1,2},{2,3},{4,5},{5,6},{6,7},{8,9},{9,10},{10,11},{12,13},{... | collective-permute-start | bytes 61448 | tf_op jit(solution)/shard_map/ppermute | solution.py:29
  209.2 3.6 %collective-permute-start.24 = (f32[5,16,1,128]{3,0,2,1:T(8,128)S(1)}, f32[5,16,1,128]{3,0,2,1:T(8,128)S(1)}, u32[]{:S(2)}, u32[]{:S(2)}) collective-permute-start(f32[5,16,1,128]{3,0,2,1:T(8,128)S(1)} %get-tuple-element.24), channel_id=1, source_target_pairs={{0,4},{4,8},{8,12},{12,16},{16,20},{20,24},{24,28},{28,32},{32,36}... | collective-permute-start | bytes 122888 | tf_op jit(solution)/shard_map/ppermute | solution.py:29
  215.3 3.2 %collective-permute-done.24 = f32[5,16,1,128]{3,0,2,1:T(8,128)S(1)} collective-permute-done((f32[5,16,1,128]{3,0,2,1:T(8,128)S(1)}, f32[5,16,1,128]{3,0,2,1:T(8,128)S(1)}, u32[]{:S(2)}, u32[]{:S(2)}) %collective-permute-start.24) | collective-permute-done | bytes 40992 | tf_op jit(solution)/shard_map/ppermute | solution.py:29
  (153 shorter events, 50.7 us)
Async XLA Ops:
  1.9 51.1 %collective-permute-start = (f32[5,1,8,128]{3,0,2,1:T(8,128)S(1)}, f32[5,1,8,128]{3,0,2,1:T(8,128)S(1)}, u32[]{:S(2)}, u32[]{:S(2)}) collective-permute-start(f32[5,1,8,128]{3,0,2,1:T(8,128)S(1)} %get-tuple-element.47), channel_id=1, source_target_pairs={{1,0},{2,1},{3,2},{5,4},{6,5},{7,6},{9,8},{10,9},{11,10},{13,12},{... | collective-permute-start | bytes 61448 | tf_op jit(solution)/shard_map/ppermute | solution.py:30
  10.8 42.2 %collective-permute-start.1 = (f32[5,1,8,128]{3,0,2,1:T(8,128)S(1)}, f32[5,1,8,128]{3,0,2,1:T(8,128)S(1)}, u32[]{:S(2)}, u32[]{:S(2)}) collective-permute-start(f32[5,1,8,128]{3,0,2,1:T(8,128)S(1)} %get-tuple-element.46), channel_id=1, source_target_pairs={{0,1},{1,2},{2,3},{4,5},{5,6},{6,7},{8,9},{9,10},{10,11},{12,13},{... | collective-permute-start | bytes 61448 | tf_op jit(solution)/shard_map/ppermute | solution.py:29
  12.7 40.9 %collective-permute-start.3 = (f32[5,16,1,128]{3,0,2,1:T(8,128)S(1)}, f32[5,16,1,128]{3,0,2,1:T(8,128)S(1)}, u32[]{:S(2)}, u32[]{:S(2)}) collective-permute-start(f32[5,16,1,128]{3,0,2,1:T(8,128)S(1)} %get-tuple-element.43), channel_id=1, source_target_pairs={{4,0},{8,4},{12,8},{16,12},{20,16},{24,20},{28,24},{32,28},{36,32}... | collective-permute-start | bytes 122888 | tf_op jit(solution)/shard_map/ppermute | solution.py:30
  24.5 26.0 %collective-permute-start.2 = (f32[5,128]{1,0:T(8,128)S(1)}, f32[5,128]{1,0:T(8,128)S(1)}, u32[]{:S(2)}, u32[]{:S(2)}) collective-permute-start(f32[5,128]{1,0:T(8,128)S(1)} %reshape_squeeze.18), channel_id=1, source_target_pairs={{0,256},{4,260},{8,264},{12,268},{16,272},{20,276},{24,280},{28,28... | collective-permute-start | bytes 7688 | tf_op jit(solution)/shard_map/ppermute | solution.py:37
  30.6 23.1 %collective-permute-start.4 = (f32[5,16,1,128]{3,0,2,1:T(8,128)S(1)}, f32[5,16,1,128]{3,0,2,1:T(8,128)S(1)}, u32[]{:S(2)}, u32[]{:S(2)}) collective-permute-start(f32[5,16,1,128]{3,0,2,1:T(8,128)S(1)} %get-tuple-element.42), channel_id=1, source_target_pairs={{0,4},{4,8},{8,12},{12,16},{16,20},{20,24},{24,28},{28,32},{32,36}... | collective-permute-start | bytes 122888 | tf_op jit(solution)/shard_map/ppermute | solution.py:29
  36.1 55.9 %all-to-all-start = ((f32[128,1,4]{2,1,0:T(1,128)}), f32[128,1,4]{2,1,0:T(1,128)S(1)}, u32[]{:S(2)}, u32[]{:S(2)}) async-start(f32[128,1,4]{2,1,0:T(1,128)} %bitcast.20), calls=%async_computation | async-start | bytes 131072 | tf_op jit(solution)/shard_map/all_to_all | solution.py:156
  55.8 25.8 %collective-permute-start.7 = (f32[5,128]{1,0:T(8,128)S(1)}, f32[5,128]{1,0:T(8,128)S(1)}, u32[]{:S(2)}, u32[]{:S(2)}) collective-permute-start(f32[5,128]{1,0:T(8,128)S(1)} %reshape_squeeze.19), channel_id=1, source_target_pairs={{0,256},{4,260},{8,264},{12,268},{16,272},{20,276},{24,280},{28,28... | collective-permute-start | bytes 7688 | tf_op jit(solution)/shard_map/ppermute | solution.py:37
  67.3 15.9 %collective-permute-start.5 = (f32[5,1,8,128]{3,0,2,1:T(8,128)S(1)}, f32[5,1,8,128]{3,0,2,1:T(8,128)S(1)}, u32[]{:S(2)}, u32[]{:S(2)}) collective-permute-start(f32[5,1,8,128]{3,0,2,1:T(8,128)S(1)} %get-tuple-element.41), channel_id=1, source_target_pairs={{1,0},{2,1},{3,2},{5,4},{6,5},{7,6},{9,8},{10,9},{11,10},{13,12},{... | collective-permute-start | bytes 61448 | tf_op jit(solution)/shard_map/ppermute | solution.py:30
  69.3 14.0 %collective-permute-start.6 = (f32[5,1,8,128]{3,0,2,1:T(8,128)S(1)}, f32[5,1,8,128]{3,0,2,1:T(8,128)S(1)}, u32[]{:S(2)}, u32[]{:S(2)}) collective-permute-start(f32[5,1,8,128]{3,0,2,1:T(8,128)S(1)} %get-tuple-element.40), channel_id=1, source_target_pairs={{0,1},{1,2},{2,3},{4,5},{5,6},{6,7},{8,9},{9,10},{10,11},{12,13},{... | collective-permute-start | bytes 61448 | tf_op jit(solution)/shard_map/ppermute | solution.py:29
  74.4 9.5 %collective-permute-start.8 = (f32[5,16,1,128]{3,0,2,1:T(8,128)S(1)}, f32[5,16,1,128]{3,0,2,1:T(8,128)S(1)}, u32[]{:S(2)}, u32[]{:S(2)}) collective-permute-start(f32[5,16,1,128]{3,0,2,1:T(8,128)S(1)} %get-tuple-element.37), channel_id=1, source_target_pairs={{4,0},{8,4},{12,8},{16,12},{20,16},{24,20},{28,24},{32,28},{36,32}... | collective-permute-start | bytes 122888 | tf_op jit(solution)/shard_map/ppermute | solution.py:30
  79.6 9.2 %collective-permute-start.9 = (f32[5,16,1,128]{3,0,2,1:T(8,128)S(1)}, f32[5,16,1,128]{3,0,2,1:T(8,128)S(1)}, u32[]{:S(2)}, u32[]{:S(2)}) collective-permute-start(f32[5,16,1,128]{3,0,2,1:T(8,128)S(1)} %get-tuple-element.36), channel_id=1, source_target_pairs={{0,4},{4,8},{8,12},{12,16},{16,20},{20,24},{24,28},{28,32},{32,36}... | collective-permute-start | bytes 122888 | tf_op jit(solution)/shard_map/ppermute | solution.py:29
  92.0 25.9 %all-to-all-start.1 = ((f32[128,4,128]{2,1,0:T(4,128)}), f32[128,4,128]{2,1,0:T(4,128)S(1)}, u32[]{:S(2)}, u32[]{:S(2)}) async-start(f32[128,4,128]{2,1,0:T(4,128)} %bitcast.23), calls=%async_computation.1 | async-start | bytes 524288 | tf_op jit(solution)/shard_map/all_to_all | solution.py:155
  119.5 40.1 %all-to-all-start.2 = ((f32[128,4,128]{2,1,0:T(4,128)}), f32[128,4,128]{2,1,0:T(4,128)S(1)}, u32[]{:S(2)}, u32[]{:S(2)}) async-start(f32[128,4,128]{2,1,0:T(4,128)} %bitcast.25), calls=%async_computation.2 | async-start | bytes 524288 | tf_op jit(solution)/shard_map/all_to_all | solution.py:163
  128.4 30.5 %collective-permute-start.10 = (f32[2,1,8,128]{3,2,1,0:T(8,128)S(1)}, f32[2,1,8,128]{3,2,1,0:T(8,128)S(1)}, u32[]{:S(2)}, u32[]{:S(2)}) collective-permute-start(f32[2,1,8,128]{3,2,1,0:T(8,128)S(1)} %get-tuple-element.60), channel_id=1, source_target_pairs={{1,0},{2,1},{3,2},{5,4},{6,5},{7,6},{9,8},{10,9},{11,10},{13,12},{... | collective-permute-start | bytes 24584 | tf_op jit(solution)/shard_map/ppermute | solution.py:30
  131.0 27.9 %collective-permute-start.12 = (f32[2,1,8,128]{3,2,1,0:T(8,128)S(1)}, f32[2,1,8,128]{3,2,1,0:T(8,128)S(1)}, u32[]{:S(2)}, u32[]{:S(2)}) collective-permute-start(f32[2,1,8,128]{3,2,1,0:T(8,128)S(1)} %get-tuple-element.61), channel_id=1, source_target_pairs={{0,1},{1,2},{2,3},{4,5},{5,6},{6,7},{8,9},{9,10},{10,11},{12,13},{... | collective-permute-start | bytes 24584 | tf_op jit(solution)/shard_map/ppermute | solution.py:29
  135.5 23.4 %collective-permute-start.18 = (f32[2,16,1,128]{3,2,1,0:T(1,128)S(1)}, f32[2,16,1,128]{3,2,1,0:T(1,128)S(1)}, u32[]{:S(2)}, u32[]{:S(2)}) collective-permute-start(f32[2,16,1,128]{3,2,1,0:T(1,128)S(1)} %get-tuple-element.57), channel_id=1, source_target_pairs={{0,4},{4,8},{8,12},{12,16},{16,20},{20,24},{24,28},{28,32},{32,36}... | collective-permute-start | bytes 49160 | tf_op jit(solution)/shard_map/ppermute | solution.py:29
  138.0 20.9 %collective-permute-start.16 = (f32[2,16,1,128]{3,2,1,0:T(1,128)S(1)}, f32[2,16,1,128]{3,2,1,0:T(1,128)S(1)}, u32[]{:S(2)}, u32[]{:S(2)}) collective-permute-start(f32[2,16,1,128]{3,2,1,0:T(1,128)S(1)} %get-tuple-element.56), channel_id=1, source_target_pairs={{4,0},{8,4},{12,8},{16,12},{20,16},{24,20},{28,24},{32,28},{36,32}... | collective-permute-start | bytes 49160 | tf_op jit(solution)/shard_map/ppermute | solution.py:30
  145.2 13.0 %collective-permute-start.14 = (f32[2,128]{1,0:T(2,128)S(1)}, f32[2,128]{1,0:T(2,128)S(1)}, u32[]{:S(2)}, u32[]{:S(2)}) collective-permute-start(f32[2,128]{1,0:T(2,128)S(1)} %reshape_squeeze.21), channel_id=1, source_target_pairs={{0,256},{4,260},{8,264},{12,268},{16,272},{20,276},{24,280},{28,28... | collective-permute-start | bytes 3080 | tf_op jit(solution)/shard_map/ppermute | solution.py:37
  162.8 22.7 %collective-permute-start.15 = (f32[5,128]{1,0:T(8,128)S(1)}, f32[5,128]{1,0:T(8,128)S(1)}, u32[]{:S(2)}, u32[]{:S(2)}) collective-permute-start(f32[5,128]{1,0:T(8,128)S(1)} %reshape_squeeze.22), channel_id=1, source_target_pairs={{0,256},{4,260},{8,264},{12,268},{16,272},{20,276},{24,280},{28,28... | collective-permute-start | bytes 7688 | tf_op jit(solution)/shard_map/ppermute | solution.py:37
  174.3 12.1 %collective-permute-start.13 = (f32[5,1,8,128]{3,0,2,1:T(8,128)S(1)}, f32[5,1,8,128]{3,0,2,1:T(8,128)S(1)}, u32[]{:S(2)}, u32[]{:S(2)}) collective-permute-start(f32[5,1,8,128]{3,0,2,1:T(8,128)S(1)} %get-tuple-element.35), channel_id=1, source_target_pairs={{0,1},{1,2},{2,3},{4,5},{5,6},{6,7},{8,9},{9,10},{10,11},{12,13},{... | collective-permute-start | bytes 61448 | tf_op jit(solution)/shard_map/ppermute | solution.py:29
  182.1 9.2 %collective-permute-start.19 = (f32[5,16,1,128]{3,0,2,1:T(8,128)S(1)}, f32[5,16,1,128]{3,0,2,1:T(8,128)S(1)}, u32[]{:S(2)}, u32[]{:S(2)}) collective-permute-start(f32[5,16,1,128]{3,0,2,1:T(8,128)S(1)} %get-tuple-element.30), channel_id=1, source_target_pairs={{0,4},{4,8},{8,12},{12,16},{16,20},{20,24},{24,28},{28,32},{32,36}... | collective-permute-start | bytes 122888 | tf_op jit(solution)/shard_map/ppermute | solution.py:29
  194.1 18.7 %collective-permute-start.22 = (f32[5,128]{1,0:T(8,128)S(1)}, f32[5,128]{1,0:T(8,128)S(1)}, u32[]{:S(2)}, u32[]{:S(2)}) collective-permute-start(f32[5,128]{1,0:T(8,128)S(1)} %reshape_squeeze.23), channel_id=1, source_target_pairs={{0,256},{4,260},{8,264},{12,268},{16,272},{20,276},{24,280},{28,28... | collective-permute-start | bytes 7688 | tf_op jit(solution)/shard_map/ppermute | solution.py:37
  197.9 15.9 %collective-permute-start.21 = (f32[5,1,8,128]{3,0,2,1:T(8,128)S(1)}, f32[5,1,8,128]{3,0,2,1:T(8,128)S(1)}, u32[]{:S(2)}, u32[]{:S(2)}) collective-permute-start(f32[5,1,8,128]{3,0,2,1:T(8,128)S(1)} %get-tuple-element.29), channel_id=1, source_target_pairs={{0,1},{1,2},{2,3},{4,5},{5,6},{6,7},{8,9},{9,10},{10,11},{12,13},{... | collective-permute-start | bytes 61448 | tf_op jit(solution)/shard_map/ppermute | solution.py:29
  209.2 9.2 %collective-permute-start.24 = (f32[5,16,1,128]{3,0,2,1:T(8,128)S(1)}, f32[5,16,1,128]{3,0,2,1:T(8,128)S(1)}, u32[]{:S(2)}, u32[]{:S(2)}) collective-permute-start(f32[5,16,1,128]{3,0,2,1:T(8,128)S(1)} %get-tuple-element.24), channel_id=1, source_target_pairs={{0,4},{4,8},{8,12},{12,16},{16,20},{20,24},{24,28},{28,32},{32,36}... | collective-permute-start | bytes 122888 | tf_op jit(solution)/shard_map/ppermute | solution.py:29
  (19 other events, 160.0 us)
where the time goes:
time: 222 us; the launch traced here: 220 us
  starting transfers between devices  154 us (69%)
  waiting for transfers between devices  30.5 us (14%)
  matrix products  16.2 us (7%)
  local copies, waits for them, and re-layouts  15.2 us (7%)
  other arithmetic  2.47 us (1%)
  between operations  2.35 us (1%)
    ppermute x10, starting transfers between devices, with_halo(): after = lax.ppermute(initial, axis, down)  44.8 us
    ppermute x5, starting transfers between devices, from_behind(): lax.ppermute(shard, axis, [(i, (i + by) % length) for i in range(length)])  44.4 us
    ppermute x10, starting transfers between devices, with_halo(): before = lax.ppermute(last, axis, up)  36.2 us
    all_to_all x1, waiting for transfers between devices, local(): lax.all_to_all(outgoing, 'sector', split_axis=0, concat_axis=0, tiled=True)  17.6 us
    all_to_all x1, starting transfers between devices, local(): lax.all_to_all(out_angle, 'sector', split_axis=0, concat_axis=0, tiled=True)  12.8 us
    ppermute x10, waiting for transfers between devices, with_halo(): before = lax.ppermute(last, axis, up)  11.5 us
    dot_general x12, matrix products, couple(): return jnp.einsum('fg,g...->f...', matrix, field, precision=PRECISE)  10.3 us
    all_to_all x1, starting transfers between devices, local(): lax.all_to_all(reply.reshape(sectors, capacity, RADII), 'sector', split_a...  8.89 us
  transfers between devices with their start and end apart: 28, of which 5 were waited for; matrix products, arithmetic and copies ran while one was open for 9% of the time, Pallas kernels for 0%

commit v1 on v0

v1 whole, which is shorter than its diff:
```python
import functools
import math

import jax
import jax.numpy as jnp
from jax import lax
from jax.experimental import pallas as pl
from jax.experimental.pallas import tpu as pltpu
from jax.sharding import PartitionSpec as P

PLANES = 16
COLS = 8
RADII = 128
PANELS = 384
ORDERS = 16
MODES = 31
SECTORS = 128
SLABS = 4
GROUPS = 4
MEMBERS = SECTORS // GROUPS
CAP = 4
SLOTS = GROUPS * CAP
ROWS = MEMBERS * SLOTS
WAVES = 32
SCALE = PANELS**-0.5
TIME_STEP = 0.25
VISCOSITY = 0.05
KEEP = 1.0 - 6.0 * VISCOSITY * TIME_STEP
SPREAD = VISCOSITY * TIME_STEP
HALF = 0.5 * TIME_STEP
MESH = pl.DeviceIdType.MESH
F32, BF16, I32 = jnp.float32, jnp.bfloat16, jnp.int32


def split(x):
    high = x.astype(BF16)
    return high, (x - high.astype(F32)).astype(BF16)


def dot(a, b):
    return lax.dot_general(a, b, (((1,), (0,)), ((), ())), preferred_element_type=F32)


def dot_nt(a, b):
    return lax.dot_general(a, b, (((1,), (1,)), ((), ())), preferred_element_type=F32)


def iota(shape, dim):
    return lax.broadcasted_iota(I32, shape, dim)


def kernel(
    state,
    mean,
    sound,
    flux_a,
    flux_r,
    flux_t,
    pair,
    weight,
    cell,
    owner,
    count,
    out,
    harm,
    q0,
    q1,
    p0,
    p1,
    col_send,
    col_recv,
    mir_send,
    mir_recv,
    pick,
    pick_t,
    factor,
    wave_out,
    wave_in,
    enc,
    enc_t,
    lines_out,
    lines_in,
    part,
    part_in,
    whole,
    grad_out,
    grad_in,
    load_sem,
    halo_send,
    halo_recv,
    many_send,
    many_recv,
    few_send,
    few_recv,
):
    sector = lax.axis_index("sector")
    slab = lax.axis_index("slab")
    group = lax.div(sector, MEMBERS)
    member = lax.rem(sector, MEMBERS)
    right = lax.rem(sector + 1, SECTORS)
    left = lax.rem(sector + SECTORS - 1, SECTORS)
    behind = lax.rem(sector + SECTORS // 2, SECTORS)

    def mate(r):
        return group * MEMBERS + lax.rem(member + r, MEMBERS)

    def twin(k):
        return lax.rem(group + k, GROUPS) * MEMBERS + member

    loads = [
        pltpu.make_async_copy(state, q0.at[pl.ds(0, 5), pl.ds(1, PLANES)], load_sem.at[0]),
        pltpu.make_async_copy(mean, q0.at[5, pl.ds(1, PLANES)], load_sem.at[1]),
        pltpu.make_async_copy(sound, q0.at[6, pl.ds(1, PLANES)], load_sem.at[2]),
    ]
    for load in loads:
        load.start()

    barrier = pltpu.get_barrier_semaphore()

    def greet(to_sector, to_slab):
        pl.semaphore_signal(barrier, inc=1, device_id=(to_sector, to_slab), device_id_type=MESH)

    greet(right, slab)
    greet(left, slab)

    @pl.when(slab > 0)
    def _():
        greet(sector, slab - 1)

    @pl.when(slab < SLABS - 1)
    def _():
        greet(sector, slab + 1)

    for k in range(1, GROUPS):
        greet(twin(k), slab)

    def greet_mate(r, carry):
        greet(mate(r), slab)
        return carry

    lax.fori_loop(1, MEMBERS, greet_mate, 0)

    row = iota((128, 128), 0)
    lane = iota((128, 128), 1)
    owners = owner[...]
    cells = cell[...]
    weights = weight[...]
    live = count[0, 0]
    across, down = [], []
    for q in range(3):
        wide = jnp.broadcast_to(owners[:, q * 128 : (q + 1) * 128], (128, 128)).astype(F32)
        across.append(wide)
        down.append(wide.T)
    slot_pieces, cell_pieces, weight_pieces = [], [], []
    tall = iota((ROWS, 128), 0)
    for q in range(3):
        earlier = jnp.where((down[q] == across[q]) & (row < lane), 1.0, 0.0)
        for s in range(q):
            earlier = earlier + jnp.where(down[s] == across[q], 1.0, 0.0)
        rank = jnp.sum(earlier, axis=0, keepdims=True).astype(I32)
        at = slice(q * 128, (q + 1) * 128)
        name = owners[:, at]
        relative = (name + MEMBERS - member) % MEMBERS
        slot = relative * SLOTS + (name // MEMBERS) * CAP + rank
        place = iota((1, 128), 1) + q * 128
        slot = jnp.where(place < live, slot, -1)
        slot_pieces.append(jnp.where(tall == slot, 1.0, 0.0).astype(BF16))
        cell_pieces.append(jnp.where(row == cells[:, at], 1.0, 0.0).astype(BF16))
        weight_pieces.append(jnp.broadcast_to(weights[:, at], (128, 128)))
    slots = jnp.concatenate(slot_pieces, axis=1)
    spots = jnp.concatenate(cell_pieces, axis=1)
    heavy, light = split(jnp.concatenate(weight_pieces, axis=1))
    picked = dot_nt(slots, spots).astype(BF16)
    pick[...] = picked
    pick_t[...] = dot_nt(spots, slots).astype(BF16)
    factor[...] = dot_nt(slots, heavy) + dot_nt(slots, light)
    order = lane % WAVES
    turn = jnp.where(order < ORDERS, order, order - (ORDERS - 1))
    turn = turn * (sector * COLS + row % COLS) + jnp.where(order < ORDERS, 0, 768)
    turn = turn % 1024
    table = jnp.cos(turn.astype(F32) * (2.0 * math.pi / 1024.0)) * SCALE
    table = jnp.where(order < MODES, table, 0.0)
    table_high, table_low = split(table)
    waves = dot(picked, table_high) + dot(picked, table_low)
    tall_lane = iota((ROWS, 128), 1)
    waves = jnp.where((tall % SLOTS) // CAP == tall_lane // WAVES, waves, 0.0)
    waves = waves.reshape(MEMBERS, SLOTS, 128)
    waves = (waves[:, :8] + waves[:, 8:]).reshape(MEMBERS * 8, 128)
    waves = waves.reshape(MEMBERS, 8, 128)
    waves = waves + jnp.concatenate([waves[:, 4:], waves[:, :4]], axis=1)
    wave_out[...] = waves

    sub = iota((8, 128), 0)
    ray = iota((8, 128), 1)
    pairs = jnp.zeros((8, 128), I32)
    for c in range(COLS):
        pairs = jnp.where(sub == c, pair[0, c], pairs)
    parity = jnp.where((ray % 8 == 2) | (ray % 8 == 3), -1.0, 1.0)

    @pl.when(slab == 0)
    def _():
        for ref in (q0, q1, p0, p1):
            ref[:, 0] = jnp.zeros_like(ref[:, 0])

    @pl.when(slab == SLABS - 1)
    def _():
        for ref in (q0, q1, p0, p1):
            ref[:, PLANES + 1] = jnp.zeros_like(ref[:, PLANES + 1])

    def pack_columns(ref, level, fields):
        flat = ref.reshape(ref.shape[0] * (PLANES + 2) * COLS, RADII)
        for f in fields:
            for side, c in ((0, 0), (1, COLS - 1)):
                begin = (f * (PLANES + 2) + 1) * COLS + c
                col_send[level, side, f * PLANES : (f + 1) * PLANES] = flat[
                    pl.ds(begin, PLANES, stride=COLS), :
                ]

    def columns_of(ref, level, phase, first, number):
        rows = pl.ds(first * PLANES, number * PLANES)
        copies = []
        for side, to in ((0, left), (1, right)):
            copies.append(
                pltpu.make_async_remote_copy(
                    src_ref=col_send.at[level, side, rows],
                    dst_ref=col_recv.at[level, side, rows],
                    send_sem=halo_send.at[phase, side],
                    recv_sem=halo_recv.at[phase, side],
                    device_id=(to, slab),
                    device_id_type=MESH,
                )
            )
        return copies

    def planes_of(ref, phase, first, number):
        fields = pl.ds(first, number)
        up = pltpu.make_async_remote_copy(
            src_ref=ref.at[fields, PLANES],
            dst_ref=ref.at[fields, 0],
            send_sem=halo_send.at[phase, 2],
            recv_sem=halo_recv.at[phase, 2],
            device_id=(sector, lax.rem(slab + 1, SLABS)),
            device_id_type=MESH,
        )
        downward = pltpu.make_async_remote_copy(
            src_ref=ref.at[fields, 1],
            dst_ref=ref.at[fields, PLANES + 1],
            send_sem=halo_send.at[phase, 3],
            recv_sem=halo_recv.at[phase, 3],
            device_id=(sector, lax.rem(slab + SLABS - 1, SLABS)),
            device_id_type=MESH,
        )
        return up, downward

    def mirror_of(level, phase):
        return pltpu.make_async_remote_copy(
            src_ref=mir_send.at[level],
            dst_ref=mir_recv.at[level],
            send_sem=halo_send.at[phase, 4],
            recv_sem=halo_recv.at[phase, 4],
            device_id=(behind, slab),
            device_id_type=MESH,
        )

    def exchange(ref, level, phase, first, number, with_mirror, act):
        for copy in columns_of(ref, level, phase, first, number):
            act(copy, "both")
        up, downward = planes_of(ref, phase, first, number)

        @pl.when(slab < SLABS - 1)
        def _():
            act(up, "send")
            act(downward, "recv")

        @pl.when(slab > 0)
        def _():
            act(downward, "send")
            act(up, "recv")

        if with_mirror:
            act(mirror_of(level, phase), "both")

    def start(copy, part_of):
        if part_of != "recv":
            copy.start()

    def arrive(copy, part_of):
        if part_of != "send":
            copy.wait_recv()

    def leave(copy, part_of):
        if part_of != "recv":
            copy.wait_send()

    def pack_mirror(i, fields, total):
        here = jnp.zeros((8, 128), F32)
        for f, value in enumerate(fields):
            here = jnp.where(ray == f, value if f == 0 else pltpu.roll(value, f, 1), here)
        return jnp.where(ray // 8 == i, pltpu.roll(here, i * 8, 1), total)

    def facing(level):
        raw = mir_recv[level]
        total = jnp.zeros((8, 128), F32)
        for c in range(COLS):
            total = jnp.where(pairs == c, jnp.broadcast_to(raw[c : c + 1], (8, 128)), total)
        return total * parity

    def at_plane(mirror, i):
        return pltpu.roll(mirror, lax.rem(128 - i * 8, 128), 1)

    def beside(value, level, f, i, inner):
        before = jnp.broadcast_to(col_recv[level, 1, pl.ds(f * PLANES + i, 1), :], (8, 128))
        after = jnp.broadcast_to(col_recv[level, 0, pl.ds(f * PLANES + i, 1), :], (8, 128))
        t_minus = jnp.where(sub == 0, before, pltpu.roll(value, 1, 0))
        t_plus = jnp.where(sub == COLS - 1, after, pltpu.roll(value, COLS - 1, 0))
        core = inner if f == 0 else pltpu.roll(inner, 128 - f, 1)
        r_minus = jnp.where(ray == 0, core, pltpu.roll(value, 1, 1))
        r_plus = jnp.where(ray == RADII - 1, 0.0, pltpu.roll(value, RADII - 1, 1))
        return t_minus, t_plus, r_minus, r_plus

    inverse = 1.0 / (ray.astype(F32) + 0.5)

    def forward_plane(src, level, dst, mirror, i, total):
        u, c = q0[5, i + 1] * HALF, q0[6, i + 1] * HALF
        inner = at_plane(mirror, i)
        values, dx, dr, dt, around = [], [], [], [], []
        for f in range(5):
            value, x_minus, x_plus = src[f, i + 1], src[f, i], src[f, i + 2]
            t_minus, t_plus, r_minus, r_plus = beside(value, level, f, i, inner)
            values.append(value)
            dx.append(x_plus - x_minus)
            dr.append(r_plus - r_minus)
            dt.append((t_plus - t_minus) * inverse)
            around.append((x_plus + x_minus) + (t_plus + t_minus) + (r_plus + r_minus))
        results = []
        for f in range(5):
            mixed = flux_a[f, 0] * dx[0] + flux_r[f, 0] * dr[0] + flux_t[f, 0] * dt[0]
            for g in range(1, 5):
                mixed = mixed + flux_a[f, g] * dx[g] + flux_r[f, g] * dr[g] + flux_t[f, g] * dt[g]
            result = values[f] * KEEP + around[f] * SPREAD - u * dx[f] - c * mixed
            dst[f, i + 1] = result
            results.append(result)
        return pack_mirror(i, results, total)

    def adjoint_plane(src, level, store, mirror, coef_mirror, i, total):
        u_minus, u_plus = q0[5, i] * HALF, q0[5, i + 2] * HALF
        c = q0[6, i + 1] * HALF
        c_minus, c_plus = q0[6, i] * HALF, q0[6, i + 2] * HALF
        before = jnp.broadcast_to(col_recv[0, 1, pl.ds(6 * PLANES + i, 1), :], (8, 128)) * HALF
        after = jnp.broadcast_to(col_recv[0, 0, pl.ds(6 * PLANES + i, 1), :], (8, 128)) * HALF
        core = pltpu.roll(at_plane(coef_mirror, i), 128 - 6, 1) * HALF
        c_t_minus = jnp.where(sub == 0, before, pltpu.roll(c, 1, 0)) * inverse
        c_t_plus = jnp.where(sub == COLS - 1, after, pltpu.roll(c, COLS - 1, 0)) * inverse
        c_r_minus = jnp.where(ray == 0, core, pltpu.roll(c, 1, 1))
        c_r_plus = pltpu.roll(c, RADII - 1, 1)
        inner = at_plane(mirror, i)
        carried, dx, dr, dt = [], [], [], []
        for f in range(5):
            value, x_minus, x_plus = src[f, i + 1], src[f, i], src[f, i + 2]
            t_minus, t_plus, r_minus, r_plus = beside(value, level, f, i, inner)
            dx.append(c_plus * x_plus - c_minus * x_minus)
            dr.append(c_r_plus * r_plus - c_r_minus * r_minus)
            dt.append(c_t_plus * t_plus - c_t_minus * t_minus)
            around = (x_plus + x_minus) + (t_plus + t_minus) + (r_plus + r_minus)
            carried.append(
                value * KEEP + around * SPREAD + (u_plus * x_plus - u_minus * x_minus)
            )
        results = []
        for f in range(5):
            result = carried[f]
            for g in range(5):
                result = result + flux_a[g, f] * dx[g] + flux_r[g, f] * dr[g] + flux_t[g, f] * dt[g]
            store(f, i, result)
            results.append(result)
        return results if total is None else pack_mirror(i, results, total)

    blank = jnp.zeros((8, 128), F32)

    for load in loads:
        load.wait()
    pack_columns(q0, 0, range(7))
    mir_send[0] = lax.fori_loop(
        0, PLANES, lambda i, total: pack_mirror(i, [q0[f, i + 1] for f in range(7)], total), blank
    )
    pl.semaphore_wait(
        barrier,
        MEMBERS - 1 + GROUPS - 1 + 2 + jnp.where(slab > 0, 1, 0) + jnp.where(slab < SLABS - 1, 1, 0),
    )
    exchange(q0, 0, 0, 0, 7, True, start)

    def to_mate(source, target, which):
        def copy_of(r):
            return pltpu.make_async_remote_copy(
                src_ref=source.at[r],
                dst_ref=target.at[r],
                send_sem=many_send.at[which],
                recv_sem=many_recv.at[which],
                device_id=(mate(r), slab),
                device_id_type=MESH,
            )

        return copy_of

    def back_mate(source, target, which):
        def copy_of(r):
            return pltpu.make_async_remote_copy(
                src_ref=source.at[r],
                dst_ref=target.at[r],
                send_sem=many_send.at[which],
                recv_sem=many_recv.at[which],
                device_id=(mate(MEMBERS - r), slab),
                device_id_type=MESH,
            )

        return copy_of

    def start_all(copy_of):
        def step(r, carry):
            copy_of(r).start()
            return carry

        lax.fori_loop(1, MEMBERS, step, 0)

    def all_of(source, target, which):
        rest = pl.ds(1, MEMBERS - 1)
        return pltpu.make_async_remote_copy(
            src_ref=source.at[rest],
            dst_ref=target.at[rest],
            send_sem=many_send.at[which],
            recv_sem=many_recv.at[which],
            device_id=(right, slab),
            device_id_type=MESH,
        )

    start_all(to_mate(wave_out, wave_in, 0))
    wave_in[0] = wave_out[0]
    exchange(q0, 0, 0, 0, 7, True, arrive)
    coef_mirror = facing(0)
    mir_send[1] = lax.fori_loop(
        0, PLANES, functools.partial(forward_plane, q0, 0, q1, coef_mirror), blank
    )
    pack_columns(q1, 1, range(5))
    exchange(q1, 1, 1, 0, 5, True, start)
    exchange(q1, 1, 1, 0, 5, True, arrive)
    mir_send[2] = lax.fori_loop(
        0, PLANES, functools.partial(forward_plane, q1, 1, p0, facing(1)), blank
    )

    pressure = p0[4, 1 : PLANES + 1].reshape(PLANES * COLS, RADII)
    high, low = split(pressure)
    lines = (dot(pick[...], high) + dot(pick[...], low)) * factor[...]
    lines_out[...] = lines.reshape(MEMBERS, SLOTS, RADII)
    start_all(to_mate(lines_out, lines_in, 1))
    lines_in[0] = lines_out[0]
    pack_columns(p0, 2, range(4))
    exchange(p0, 2, 2, 0, 4, False, start)
    all_of(wave_out, wave_in, 0).wait_recv()
    given = wave_in[...]
    sub3, ray3 = iota((MEMBERS, 8, 128), 1), iota((MEMBERS, 8, 128), 2)
    first = jnp.where(sub3 // CAP == ray3 // WAVES, given, 0.0)
    second = jnp.where(sub3 // CAP + 2 == ray3 // WAVES, given, 0.0)
    encoder = jnp.concatenate([first, second], axis=1).reshape(ROWS, 128)
    enc[0], enc[1] = split(encoder)
    enc_t[0], enc_t[1] = split(encoder.T)

    all_of(lines_out, lines_in, 1).wait_recv()
    high, low = split(lines_in[...].reshape(ROWS, RADII))
    part[...] = dot(enc_t[0], high) + (dot(enc_t[0], low) + dot(enc_t[1], high))

    def to_twin(k):
        return pltpu.make_async_remote_copy(
            src_ref=part.at[pl.ds(pl.multiple_of(lax.rem(group + k, GROUPS) * WAVES, WAVES), WAVES)],
            dst_ref=part_in.at[k - 1],
            send_sem=few_send.at[0, k - 1],
            recv_sem=few_recv.at[0, k - 1],
            device_id=(twin(k), slab),
            device_id_type=MESH,
        )

    own_rows = pl.ds(pl.multiple_of(group * WAVES, WAVES), WAVES)

    def from_owner(k):
        return pltpu.make_async_remote_copy(
            src_ref=whole.at[own_rows],
            dst_ref=whole.at[own_rows],
            send_sem=few_send.at[1, k - 1],
            recv_sem=few_recv.at[1, k - 1],
            device_id=(twin(k), slab),
            device_id_type=MESH,
        )

    for k in range(1, GROUPS):
        to_twin(k).start()
    mine = part[own_rows, :]
    for k in range(1, GROUPS):
        to_twin(k).wait_recv()
        mine = mine + part_in[k - 1]
    whole[own_rows, :] = mine
    for k in range(1, GROUPS):
        from_owner(k).start()
    harm[0, 0] = mine[:MODES]
    for k in range(1, GROUPS):
        from_owner(k).wait_recv()

    high, low = split(whole[...])
    grad = dot(enc[0], high) + (dot(enc[0], low) + dot(enc[1], high))
    grad_out[...] = grad.reshape(MEMBERS, SLOTS, RADII)
    start_all(back_mate(grad_out, grad_in, 2))
    grad_in[0] = grad_out[0]
    exchange(p0, 2, 2, 0, 4, False, arrive)
    all_of(grad_out, grad_in, 2).wait_recv()
    high, low = split(grad_in[...].reshape(ROWS, RADII) * factor[...])
    impulse = dot(pick_t[...], high) + dot(pick_t[...], low)
    impulse = impulse.reshape(PLANES, COLS, RADII)
    p0[4, 1 : PLANES + 1] = p0[4, 1 : PLANES + 1] + impulse

    mir_send[2] = lax.fori_loop(
        0, PLANES, lambda i, total: pack_mirror(i, [p0[f, i + 1] for f in range(5)], total), blank
    )
    pack_columns(p0, 2, (4,))
    exchange(p0, 2, 3, 4, 1, True, start)
    exchange(p0, 2, 3, 4, 1, True, arrive)

    def store_p1(f, i, value):
        p1[f, i + 1] = value

    def store_out(f, i, value):
        out[f, i] = value

    mirror = facing(2)
    mir_send[3] = lax.fori_loop(
        0,
        PLANES,
        lambda i, total: adjoint_plane(p0, 2, store_p1, mirror, coef_mirror, i, total),
        blank,
    )
    pack_columns(p1, 3, range(5))
    exchange(p1, 3, 4, 0, 5, True, start)
    exchange(p1, 3, 4, 0, 5, True, arrive)
    last_mirror = facing(3)

    def finish(i, carry):
        adjoint_plane(p1, 3, store_out, last_mirror, coef_mirror, i, None)
        return carry

    lax.fori_loop(0, PLANES, finish, 0)

    exchange(q0, 0, 0, 0, 7, True, leave)
    exchange(q1, 1, 1, 0, 5, True, leave)
    exchange(p0, 2, 2, 0, 4, False, leave)
    exchange(p0, 2, 3, 4, 1, True, leave)
    exchange(p1, 3, 4, 0, 5, True, leave)
    all_of(wave_out, wave_in, 0).wait_send()
    all_of(lines_out, lines_in, 1).wait_send()
    all_of(grad_out, grad_in, 2).wait_send()
    for k in range(1, GROUPS):
        to_twin(k).wait_send()
        from_owner(k).wait_send()


def local(
    state,
    mean_velocity,
    sound_speed,
    flux_axial,
    flux_radial,
    flux_azimuthal,
    axis_pair,
    panel_weight,
    panel_cell,
    panel_owner,
    panel_count,
):
    anywhere = pl.BlockSpec(memory_space=pl.ANY)
    scalar = pl.BlockSpec(memory_space=pltpu.SMEM)
    vector = pl.BlockSpec(memory_space=pltpu.VMEM)

    def grid_of(fields):
        return pltpu.VMEM((fields, PLANES + 2, COLS, RADII), F32)

    return pl.pallas_call(
        kernel,
        out_shape=(
            jax.ShapeDtypeStruct((5, PLANES, COLS, RADII), F32),
            jax.ShapeDtypeStruct((1, 1, MODES, RADII), F32),
        ),
        in_specs=[anywhere] * 3 + [scalar] * 4 + [vector] * 3 + [scalar],
        out_specs=(vector, vector),
        scratch_shapes=[
            grid_of(7),
            grid_of(5),
            grid_of(5),
            grid_of(5),
            pltpu.VMEM((4, 2, 7 * PLANES, RADII), F32),
            pltpu.VMEM((4, 2, 7 * PLANES, RADII), F32),
            pltpu.VMEM((4, 8, 128), F32),
            pltpu.VMEM((4, 8, 128), F32),
            pltpu.VMEM((ROWS, 128), BF16),
            pltpu.VMEM((128, ROWS), BF16),
            pltpu.VMEM((ROWS, 128), F32),
            pltpu.VMEM((MEMBERS, 8, 128), F32),
            pltpu.VMEM((MEMBERS, 8, 128), F32),
            pltpu.VMEM((2, ROWS, 128), BF16),
            pltpu.VMEM((2, 128, ROWS), BF16),
            pltpu.VMEM((MEMBERS, SLOTS, RADII), F32),
            pltpu.VMEM((MEMBERS, SLOTS, RADII), F32),
            pltpu.VMEM((GROUPS * WAVES, RADII), F32),
            pltpu.VMEM((GROUPS - 1, WAVES, RADII), F32),
            pltpu.VMEM((GROUPS * WAVES, RADII), F32),
            pltpu.VMEM((MEMBERS, SLOTS, RADII), F32),
            pltpu.VMEM((MEMBERS, SLOTS, RADII), F32),
            pltpu.SemaphoreType.DMA((3,)),
            pltpu.SemaphoreType.DMA((5, 5)),
            pltpu.SemaphoreType.DMA((5, 5)),
            pltpu.SemaphoreType.DMA((3,)),
            pltpu.SemaphoreType.DMA((3,)),
            pltpu.SemaphoreType.DMA((2, GROUPS - 1)),
            pltpu.SemaphoreType.DMA((2, GROUPS - 1)),
        ],
        compiler_params=pltpu.CompilerParams(
            collective_id=0, has_side_effects=True, vmem_limit_bytes=32 << 20
        ),
    )(
        state,
        mean_velocity,
        sound_speed,
        flux_axial,
        flux_radial,
        flux_azimuthal,
        axis_pair,
        panel_weight,
        panel_cell,
        panel_owner.reshape(1, PANELS),
        panel_count,
    )


def solution(mesh):
    return jax.shard_map(
        local,
        mesh=mesh,
        in_specs=(
            P(None, "slab", "sector", None),
            P("slab", "sector", None),
            P("slab", "sector", None),
            P(),
            P(),
            P(),
            P("sector", None),
            P("slab", "sector"),
            P("slab", "sector"),
            P("slab", "sector", None),
            P("slab", "sector"),
        ),
        out_specs=(P(None, "slab", "sector", None), P("slab", "sector", None, None)),
        check_vma=False,
    )
```

time: 222 us -> 106 us (0.48)
  starting transfers between devices: 154 us -> 0 us
  Pallas kernels: 0 us -> 95.9 us
  waiting for transfers between devices: 30.5 us -> 0 us
  matrix products: 16.2 us -> 0 us
  local copies, waits for them, and re-layouts: 15.2 us -> 7.37 us
  other arithmetic: 2.47 us -> 0 us
    ppermute x25 -> x0, starting transfers between devices: 125 us -> none  [the longest x10 44.8 us: with_halo(): after = lax.ppermute(initial, axis, down)]
    pallas_call x0 -> x1, Pallas kernels: none -> 95.9 us  [local(): pl.pallas_call(kernel, out_shape=(jax.ShapeDtypeStruct((5, PLANES, COLS,...]
    all_to_all x3 -> x0, starting transfers between devices: 28.2 us -> none  [the longest x1 12.8 us: local(): lax.all_to_all(out_angle, 'sector', split_axis=0, concat_axis=0, tiled=True)]
    all_to_all x3 -> x0, waiting for transfers between devices: 17.6 us -> none  [the longest x1 17.6 us: local(): lax.all_to_all(outgoing, 'sector', split_axis=0, concat_axis=0, tiled=True)]
    dot_general x24 -> x0, matrix products: 16.2 us -> none  [the longest x12 10.3 us: couple(): return jnp.einsum('fg,g...->f...', matrix, field, precision=PRECISE)]
    ppermute x25 -> x0, waiting for transfers between devices: 13 us -> none  [the longest x10 11.5 us: with_halo(): before = lax.ppermute(last, axis, up)]
    slice x17 -> x0, local copies, waits for them, and re-layouts: 2.77 us -> none  [the longest x4 1.8 us: neighbours(): inner_row = field[..., 0].reshape(fields, planes * columns)]
    broadcast_in_dim x5 -> x0, local copies, waits for them, and re-layouts: 2.49 us -> none  [neighbours(): r_minus = jnp.concatenate([mirror[..., None], field[..., :-1]], 3)]
  transfers between devices with their start and end apart: 28 -> 0, of which waited for: 5 -> 0; matrix products, arithmetic and copies ran while one was open for 9% -> 0% of each run, Pallas kernels for 0% -> 0%
where the time goes in v1:
time: 106 us; the launch traced here: 105 us
  Pallas kernels  95.9 us (90%)
  local copies, waits for them, and re-layouts  7.37 us (7%)
  between operations  1.35 us (1%)
    pallas_call x1, Pallas kernels, local(): pl.pallas_call(kernel, out_shape=(jax.ShapeDtypeStruct((5, PLANES, COLS,...  95.9 us
    unnamed x21, local copies, waits for them, and re-layouts  6.75 us

profile of v1, /device:TPU:1, one launch (start us, length us, event | category | flops | bytes accessed | tf_op | source)
XLA Modules:
  0.0 104.6 jit_solution(6528553940809879108)
XLA Ops:
  0.6 0.0 copy-start.7
  0.6 0.0 copy-start.6
  1.3 0.0 copy-start.9
  1.3 0.0 copy-done.7
  1.3 0.0 copy-done.6
  1.3 0.6 copy-done.9
  2.0 0.0 copy-start
  2.0 1.0 copy-done
  2.9 0.0 copy-start.1
  3.0 0.8 copy-done.1
  3.8 0.0 copy-start.2
  3.8 0.8 copy-done.2
  4.6 0.0 copy-start.3
  4.6 0.7 copy-done.3
  5.3 0.0 copy-start.4
  5.3 0.7 copy-done.4
  6.0 0.0 copy-start.5
  6.0 0.7 copy-done.5
  6.7 0.0 copy-start.8
  6.7 0.7 copy-done.8
  7.4 95.9 %shard_map.122 = (f32[5,16,8,128]{3,2,1,0:T(8,128)S(1)}, f32[1,1,31,128]{3,2,1,0:T(8,128)S(1)}) custom-call(f32[5,16,8,128]{3,2,1,0:T(8,128)S(1)} %copy-done, f32[16,8,128]{2,1,0:T(8,128)S(1)} %copy-done.1, f32[16,8,128]{2,1,0:T(8,128)S(1)} %copy-done.2, f32[5,5]{1,0:T(8,128)S(1)} %copy-done.3, f32[5,5]{1,0:T(8,128)S(1)} %copy-done.4, f32[5,5]{1,0:T(8,128)S(1)} %copy-done.5, ...), custom_call_target="tpu_custom_call" | custom-call | tf_op jit(solution)/shard_map/pallas_call | solution.py:581
  103.3 0.6 copy.13
  103.9 0.7 copy.16
Async XLA Ops:
  0.6 0.7 copy-start.7
  0.6 0.7 copy-start.6
  1.3 0.7 copy-start.9
  2.0 1.0 copy-start
  2.9 0.8 copy-start.1
  3.8 0.8 copy-start.2
  4.6 0.7 copy-start.3
  5.3 0.7 copy-start.4
  6.0 0.7 copy-start.5
  6.7 0.7 copy-start.8

commit v2 on v1

--- a/solution.py
+++ b/solution.py
@@ -16,18 +16,21 @@
 MODES = 31
 SECTORS = 128
 SLABS = 4
-GROUPS = 4
+GROUPS = 8
 MEMBERS = SECTORS // GROUPS
 CAP = 4
 SLOTS = GROUPS * CAP
 ROWS = MEMBERS * SLOTS
 WAVES = 32
+LANES = GROUPS * WAVES
 SCALE = PANELS**-0.5
 TIME_STEP = 0.25
 VISCOSITY = 0.05
 KEEP = 1.0 - 6.0 * VISCOSITY * TIME_STEP
 SPREAD = VISCOSITY * TIME_STEP
 HALF = 0.5 * TIME_STEP
+UNROLL = 4
+VMEM_GRANT = 60 << 20
 MESH = pl.DeviceIdType.MESH
 F32, BF16, I32 = jnp.float32, jnp.bfloat16, jnp.int32
 
@@ -57,9 +60,9 @@
     flux_r,
     flux_t,
     pair,
-    weight,
-    cell,
-    owner,
+    weight_in,
+    cell_in,
+    owner_in,
     count,
     out,
     harm,
@@ -67,10 +70,15 @@
     q1,
     p0,
     p1,
+    weight,
+    cell,
+    owner,
     col_send,
     col_recv,
     mir_send,
     mir_recv,
+    rows0,
+    turned,
     pick,
     pick_t,
     factor,
@@ -88,6 +96,7 @@
     load_sem,
     halo_send,
     halo_recv,
+    mirror_sems,
     many_send,
     many_recv,
     few_send,
@@ -112,8 +121,15 @@
         pltpu.make_async_copy(mean, q0.at[5, pl.ds(1, PLANES)], load_sem.at[1]),
         pltpu.make_async_copy(sound, q0.at[6, pl.ds(1, PLANES)], load_sem.at[2]),
     ]
-    for load in loads:
+    lists = [
+        pltpu.make_async_copy(weight_in, weight, load_sem.at[3]),
+        pltpu.make_async_copy(cell_in, cell, load_sem.at[4]),
+        pltpu.make_async_copy(owner_in, owner, load_sem.at[5]),
+    ]
+    for load in lists + loads:
         load.start()
+
+    sent = []
 
     barrier = pltpu.get_barrier_semaphore()
 
@@ -142,6 +158,8 @@
 
     row = iota((128, 128), 0)
     lane = iota((128, 128), 1)
+    for load in lists:
+        load.wait()
     owners = owner[...]
     cells = cell[...]
     weights = weight[...]
@@ -174,28 +192,57 @@
     pick[...] = picked
     pick_t[...] = dot_nt(spots, slots).astype(BF16)
     factor[...] = dot_nt(slots, heavy) + dot_nt(slots, light)
-    order = lane % WAVES
+    spread_row, spread_lane = iota((128, LANES), 0), iota((128, LANES), 1)
+    order = spread_lane % WAVES
     turn = jnp.where(order < ORDERS, order, order - (ORDERS - 1))
-    turn = turn * (sector * COLS + row % COLS) + jnp.where(order < ORDERS, 0, 768)
+    turn = turn * (sector * COLS + spread_row % COLS) + jnp.where(order < ORDERS, 0, 768)
     turn = turn % 1024
     table = jnp.cos(turn.astype(F32) * (2.0 * math.pi / 1024.0)) * SCALE
     table = jnp.where(order < MODES, table, 0.0)
     table_high, table_low = split(table)
     waves = dot(picked, table_high) + dot(picked, table_low)
-    tall_lane = iota((ROWS, 128), 1)
+    tall, tall_lane = iota((ROWS, LANES), 0), iota((ROWS, LANES), 1)
     waves = jnp.where((tall % SLOTS) // CAP == tall_lane // WAVES, waves, 0.0)
-    waves = waves.reshape(MEMBERS, SLOTS, 128)
-    waves = (waves[:, :8] + waves[:, 8:]).reshape(MEMBERS * 8, 128)
-    waves = waves.reshape(MEMBERS, 8, 128)
-    waves = waves + jnp.concatenate([waves[:, 4:], waves[:, :4]], axis=1)
-    wave_out[...] = waves
+    waves = waves.reshape(MEMBERS, SLOTS, LANES)
+    halves = waves[:, :8]
+    for h in range(1, SLOTS // 8):
+        halves = halves + waves[:, h * 8 : (h + 1) * 8]
+    wave_out[...] = halves + jnp.concatenate([halves[:, 4:], halves[:, :4]], axis=1)
 
     sub = iota((8, 128), 0)
     ray = iota((8, 128), 1)
-    pairs = jnp.zeros((8, 128), I32)
+    pairs = jnp.zeros((1, 128), I32)
     for c in range(COLS):
-        pairs = jnp.where(sub == c, pair[0, c], pairs)
-    parity = jnp.where((ray % 8 == 2) | (ray % 8 == 3), -1.0, 1.0)
+        pairs = jnp.where(lane[:1] % COLS == c, pair[0, c], pairs)
+    parity = jnp.where((sub == 2) | (sub == 3), -1.0, 1.0)
+
+    def crossing(columns):
+        meets = (row % COLS == columns) & (row // COLS == lane // COLS)
+        return jnp.where(meets, 1.0, 0.0).astype(BF16)
+
+    cross = crossing(pairs)
+
+    def across_axis(fields, matrix):
+        high, low = split(fields)
+        return dot(high, matrix) + dot(low, matrix)
+
+    def matrix_columns(entry):
+        columns = []
+        for g in range(5):
+            column = jnp.zeros((8, 128), F32)
+            for f in range(5):
+                column = jnp.where(sub == f, entry(f, g), column)
+            columns.append(column)
+        return columns
+
+    radial = matrix_columns(lambda f, g: flux_r[f, g] * HALF)
+    radial_t = matrix_columns(lambda f, g: -flux_r[g, f] * HALF)
+
+    def met(columns, mirrored, speed):
+        total = columns[0] * mirrored[:1]
+        for g in range(1, 5):
+            total = total + columns[g] * mirrored[g : g + 1]
+        return jnp.where(sub < 5, mirrored * SPREAD + total * speed, 0.0)
 
     @pl.when(slab == 0)
     def _():
@@ -252,17 +299,21 @@
         )
         return up, downward
 
-    def mirror_of(level, phase):
+    def mirror_of(level):
         return pltpu.make_async_remote_copy(
             src_ref=mir_send.at[level],
             dst_ref=mir_recv.at[level],
-            send_sem=halo_send.at[phase, 4],
-            recv_sem=halo_recv.at[phase, 4],
+            send_sem=mirror_sems.at[0, level],
+            recv_sem=mirror_sems.at[1, level],
             device_id=(behind, slab),
             device_id_type=MESH,
         )
 
-    def exchange(ref, level, phase, first, number, with_mirror, act):
+    def send_mirror(level):
+        mirror_of(level).start()
+        sent.append(lambda: mirror_of(level).wait_send())
+
+    def exchange(ref, level, phase, first, number, act):
         for copy in columns_of(ref, level, phase, first, number):
             act(copy, "both")
         up, downward = planes_of(ref, phase, first, number)
@@ -277,9 +328,6 @@
             act(downward, "send")
             act(up, "recv")
 
-        if with_mirror:
-            act(mirror_of(level, phase), "both")
-
     def start(copy, part_of):
         if part_of != "recv":
             copy.start()
@@ -292,37 +340,46 @@
         if part_of != "recv":
             copy.wait_send()
 
-    def pack_mirror(i, fields, total):
+    def pack_inner(i, fields):
         here = jnp.zeros((8, 128), F32)
         for f, value in enumerate(fields):
             here = jnp.where(ray == f, value if f == 0 else pltpu.roll(value, f, 1), here)
-        return jnp.where(ray // 8 == i, pltpu.roll(here, i * 8, 1), total)
-
-    def facing(level):
-        raw = mir_recv[level]
-        total = jnp.zeros((8, 128), F32)
-        for c in range(COLS):
-            total = jnp.where(pairs == c, jnp.broadcast_to(raw[c : c + 1], (8, 128)), total)
-        return total * parity
-
-    def at_plane(mirror, i):
-        return pltpu.roll(mirror, lax.rem(128 - i * 8, 128), 1)
+        rows0[i] = here
+
+    def packed():
+        return rows0[...].reshape(128, 128).T[:8]
+
+    def unpack(fields):
+        wide = jnp.concatenate([fields, jnp.zeros((120, 128), F32)], axis=0)
+        turned[...] = wide.T.reshape(PLANES, COLS, 128)
+
+    def lane_zero(inner, f):
+        return inner if f == 0 else pltpu.roll(inner, 128 - f, 1)
+
+    def add_inner(ref):
+        def step(i, carry):
+            inner = turned[i]
+            for f in range(5):
+                ref[f, i + 1] += jnp.where(ray == 0, lane_zero(inner, f), 0.0)
+            return carry
+
+        lax.fori_loop(0, PLANES, step, 0, unroll=4)
 
     def beside(value, level, f, i, inner):
         before = jnp.broadcast_to(col_recv[level, 1, pl.ds(f * PLANES + i, 1), :], (8, 128))
         after = jnp.broadcast_to(col_recv[level, 0, pl.ds(f * PLANES + i, 1), :], (8, 128))
         t_minus = jnp.where(sub == 0, before, pltpu.roll(value, 1, 0))
         t_plus = jnp.where(sub == COLS - 1, after, pltpu.roll(value, COLS - 1, 0))
-        core = inner if f == 0 else pltpu.roll(inner, 128 - f, 1)
+        core = 0.0 if inner is None else lane_zero(inner, f)
         r_minus = jnp.where(ray == 0, core, pltpu.roll(value, 1, 1))
         r_plus = jnp.where(ray == RADII - 1, 0.0, pltpu.roll(value, RADII - 1, 1))
         return t_minus, t_plus, r_minus, r_plus
 
     inverse = 1.0 / (ray.astype(F32) + 0.5)
 
-    def forward_plane(src, level, dst, mirror, i, total):
+    def forward_plane(src, level, dst, mirrored, i):
         u, c = q0[5, i + 1] * HALF, q0[6, i + 1] * HALF
-        inner = at_plane(mirror, i)
+        inner = turned[i] if mirrored else None
         values, dx, dr, dt, around = [], [], [], [], []
         for f in range(5):
             value, x_minus, x_plus = src[f, i + 1], src[f, i], src[f, i + 2]
@@ -340,20 +397,20 @@
             result = values[f] * KEEP + around[f] * SPREAD - u * dx[f] - c * mixed
             dst[f, i + 1] = result
             results.append(result)
-        return pack_mirror(i, results, total)
-
-    def adjoint_plane(src, level, store, mirror, coef_mirror, i, total):
+        pack_inner(i, results)
+
+    def adjoint_plane(src, level, store, mirrored, i):
         u_minus, u_plus = q0[5, i] * HALF, q0[5, i + 2] * HALF
         c = q0[6, i + 1] * HALF
         c_minus, c_plus = q0[6, i] * HALF, q0[6, i + 2] * HALF
         before = jnp.broadcast_to(col_recv[0, 1, pl.ds(6 * PLANES + i, 1), :], (8, 128)) * HALF
         after = jnp.broadcast_to(col_recv[0, 0, pl.ds(6 * PLANES + i, 1), :], (8, 128)) * HALF
-        core = pltpu.roll(at_plane(coef_mirror, i), 128 - 6, 1) * HALF
+        inner = turned[i] if mirrored else None
         c_t_minus = jnp.where(sub == 0, before, pltpu.roll(c, 1, 0)) * inverse
         c_t_plus = jnp.where(sub == COLS - 1, after, pltpu.roll(c, COLS - 1, 0)) * inverse
+        core = lane_zero(inner, 5) * HALF if mirrored else 0.0
         c_r_minus = jnp.where(ray == 0, core, pltpu.roll(c, 1, 1))
         c_r_plus = pltpu.roll(c, RADII - 1, 1)
-        inner = at_plane(mirror, i)
         carried, dx, dr, dt = [], [], [], []
         for f in range(5):
             value, x_minus, x_plus = src[f, i + 1], src[f, i], src[f, i + 2]
@@ -372,21 +429,29 @@
                 result = result + flux_a[g, f] * dx[g] + flux_r[g, f] * dr[g] + flux_t[g, f] * dt[g]
             store(f, i, result)
             results.append(result)
-        return results if total is None else pack_mirror(i, results, total)
-
-    blank = jnp.zeros((8, 128), F32)
+        if not mirrored:
+            pack_inner(i, results)
+
+    def planes(body):
+        def step(i, carry):
+            body(i)
+            return carry
+
+        lax.fori_loop(0, PLANES, step, 0, unroll=UNROLL)
 
     for load in loads:
         load.wait()
     pack_columns(q0, 0, range(7))
-    mir_send[0] = lax.fori_loop(
-        0, PLANES, lambda i, total: pack_mirror(i, [q0[f, i + 1] for f in range(7)], total), blank
-    )
+    planes(lambda i: pack_inner(i, [q0[f, i + 1] for f in (0, 1, 2, 3, 4, 6)]))
+    first_rows = jnp.where(sub == 6, pairs.astype(F32), packed())
+    mir_send[0] = first_rows
     pl.semaphore_wait(
         barrier,
         MEMBERS - 1 + GROUPS - 1 + 2 + jnp.where(slab > 0, 1, 0) + jnp.where(slab < SLABS - 1, 1, 0),
     )
-    exchange(q0, 0, 0, 0, 7, True, start)
+    send_mirror(0)
+    exchange(q0, 0, 0, 0, 7, start)
+    sent.append(lambda: exchange(q0, 0, 0, 0, 7, leave))
 
     def to_mate(source, target, which):
         def copy_of(r):
@@ -433,33 +498,48 @@
         )
 
     start_all(to_mate(wave_out, wave_in, 0))
+    sent.append(lambda: all_of(wave_out, wave_in, 0).wait_send())
     wave_in[0] = wave_out[0]
-    exchange(q0, 0, 0, 0, 7, True, arrive)
-    coef_mirror = facing(0)
-    mir_send[1] = lax.fori_loop(
-        0, PLANES, functools.partial(forward_plane, q0, 0, q1, coef_mirror), blank
-    )
+    exchange(q0, 0, 0, 0, 7, arrive)
+    planes(functools.partial(forward_plane, q0, 0, q1, False))
+    mir_send[1] = packed()
+    send_mirror(1)
+    mirror_of(0).wait_recv()
+    theirs = mir_recv[0]
+    mirrored = across_axis(theirs, cross)
+    core_speed = mirrored[5:6]
+    unpack(met(radial, mirrored * parity, first_rows[5:6]))
+    add_inner(q1)
     pack_columns(q1, 1, range(5))
-    exchange(q1, 1, 1, 0, 5, True, start)
-    exchange(q1, 1, 1, 0, 5, True, arrive)
-    mir_send[2] = lax.fori_loop(
-        0, PLANES, functools.partial(forward_plane, q1, 1, p0, facing(1)), blank
-    )
+    exchange(q1, 1, 1, 0, 5, start)
+    sent.append(lambda: exchange(q1, 1, 1, 0, 5, leave))
+    cross_back = crossing(theirs[6:7].astype(I32))
+    there = across_axis(first_rows, cross_back)
+    core_speed_there = there[5:6]
+    addition = met(radial, there * parity, theirs[5:6])
+    mirror_of(1).wait_recv()
+    unpack(across_axis(mir_recv[1] + addition, cross) * parity)
+    exchange(q1, 1, 1, 0, 5, arrive)
+    planes(functools.partial(forward_plane, q1, 1, p0, True))
 
     pressure = p0[4, 1 : PLANES + 1].reshape(PLANES * COLS, RADII)
     high, low = split(pressure)
     lines = (dot(pick[...], high) + dot(pick[...], low)) * factor[...]
     lines_out[...] = lines.reshape(MEMBERS, SLOTS, RADII)
     start_all(to_mate(lines_out, lines_in, 1))
+    sent.append(lambda: all_of(lines_out, lines_in, 1).wait_send())
     lines_in[0] = lines_out[0]
+    forward_rows = packed()
     pack_columns(p0, 2, range(4))
-    exchange(p0, 2, 2, 0, 4, False, start)
+    exchange(p0, 2, 2, 0, 4, start)
+    sent.append(lambda: exchange(p0, 2, 2, 0, 4, leave))
     all_of(wave_out, wave_in, 0).wait_recv()
     given = wave_in[...]
-    sub3, ray3 = iota((MEMBERS, 8, 128), 1), iota((MEMBERS, 8, 128), 2)
-    first = jnp.where(sub3 // CAP == ray3 // WAVES, given, 0.0)
-    second = jnp.where(sub3 // CAP + 2 == ray3 // WAVES, given, 0.0)
-    encoder = jnp.concatenate([first, second], axis=1).reshape(ROWS, 128)
+    sub3, ray3 = iota((MEMBERS, 8, LANES), 1), iota((MEMBERS, 8, LANES), 2)
+    quarters = []
+    for h in range(SLOTS // 8):
+        quarters.append(jnp.where(sub3 // CAP + 2 * h == ray3 // WAVES, given, 0.0))
+    encoder = jnp.concatenate(quarters, axis=1).reshape(ROWS, LANES)
     enc[0], enc[1] = split(encoder)
     enc_t[0], enc_t[1] = split(encoder.T)
 
@@ -491,6 +571,7 @@
 
     for k in range(1, GROUPS):
         to_twin(k).start()
+        sent.append(lambda k=k: to_twin(k).wait_send())
     mine = part[own_rows, :]
     for k in range(1, GROUPS):
         to_twin(k).wait_recv()
@@ -498,6 +579,7 @@
     whole[own_rows, :] = mine
     for k in range(1, GROUPS):
         from_owner(k).start()
+        sent.append(lambda k=k: from_owner(k).wait_send())
     harm[0, 0] = mine[:MODES]
     for k in range(1, GROUPS):
         from_owner(k).wait_recv()
@@ -506,20 +588,23 @@
     grad = dot(enc[0], high) + (dot(enc[0], low) + dot(enc[1], high))
     grad_out[...] = grad.reshape(MEMBERS, SLOTS, RADII)
     start_all(back_mate(grad_out, grad_in, 2))
+    sent.append(lambda: all_of(grad_out, grad_in, 2).wait_send())
     grad_in[0] = grad_out[0]
-    exchange(p0, 2, 2, 0, 4, False, arrive)
+    exchange(p0, 2, 2, 0, 4, arrive)
     all_of(grad_out, grad_in, 2).wait_recv()
     high, low = split(grad_in[...].reshape(ROWS, RADII) * factor[...])
     impulse = dot(pick_t[...], high) + dot(pick_t[...], low)
     impulse = impulse.reshape(PLANES, COLS, RADII)
     p0[4, 1 : PLANES + 1] = p0[4, 1 : PLANES + 1] + impulse
 
-    mir_send[2] = lax.fori_loop(
-        0, PLANES, lambda i, total: pack_mirror(i, [p0[f, i + 1] for f in range(5)], total), blank
-    )
+    pressure = p0[4, 1 : PLANES + 1].reshape(PLANES * COLS, RADII)
+    start_rows = jnp.where(sub == 4, pressure.T[:1], forward_rows)
+    mir_send[2] = start_rows
+    send_mirror(2)
     pack_columns(p0, 2, (4,))
-    exchange(p0, 2, 3, 4, 1, True, start)
-    exchange(p0, 2, 3, 4, 1, True, arrive)
+    exchange(p0, 2, 3, 4, 1, start)
+    sent.append(lambda: exchange(p0, 2, 3, 4, 1, leave))
+    exchange(p0, 2, 3, 4, 1, arrive)
 
     def store_p1(f, i, value):
         p1[f, i + 1] = value
@@ -527,35 +612,26 @@
     def store_out(f, i, value):
         out[f, i] = value
 
-    mirror = facing(2)
-    mir_send[3] = lax.fori_loop(
-        0,
-        PLANES,
-        lambda i, total: adjoint_plane(p0, 2, store_p1, mirror, coef_mirror, i, total),
-        blank,
-    )
+    planes(functools.partial(adjoint_plane, p0, 2, store_p1, False))
+    mir_send[3] = packed()
+    send_mirror(3)
+    there = across_axis(start_rows, cross_back) * parity
+    addition = met(radial_t, there, core_speed_there)
+    mirror_of(2).wait_recv()
+    mirrored = across_axis(mir_recv[2], cross) * parity
+    unpack(met(radial_t, mirrored, core_speed))
+    add_inner(p1)
     pack_columns(p1, 3, range(5))
-    exchange(p1, 3, 4, 0, 5, True, start)
-    exchange(p1, 3, 4, 0, 5, True, arrive)
-    last_mirror = facing(3)
-
-    def finish(i, carry):
-        adjoint_plane(p1, 3, store_out, last_mirror, coef_mirror, i, None)
-        return carry
-
-    lax.fori_loop(0, PLANES, finish, 0)
-
-    exchange(q0, 0, 0, 0, 7, True, leave)
-    exchange(q1, 1, 1, 0, 5, True, leave)
-    exchange(p0, 2, 2, 0, 4, False, leave)
-    exchange(p0, 2, 3, 4, 1, True, leave)
-    exchange(p1, 3, 4, 0, 5, True, leave)
-    all_of(wave_out, wave_in, 0).wait_send()
-    all_of(lines_out, lines_in, 1).wait_send()
-    all_of(grad_out, grad_in, 2).wait_send()
-    for k in range(1, GROUPS):
-        to_twin(k).wait_send()
-        from_owner(k).wait_send()
+    exchange(p1, 3, 4, 0, 5, start)
+    sent.append(lambda: exchange(p1, 3, 4, 0, 5, leave))
+    mirror_of(3).wait_recv()
+    mirrored = across_axis(mir_recv[3] + addition, cross) * parity
+    unpack(jnp.where(sub == 5, core_speed, mirrored))
+    exchange(p1, 3, 4, 0, 5, arrive)
+    planes(functools.partial(adjoint_plane, p1, 3, store_out, True))
+
+    for wait in sent:
+        wait()
 
 
 def local(
@@ -584,24 +660,29 @@
             jax.ShapeDtypeStruct((5, PLANES, COLS, RADII), F32),
             jax.ShapeDtypeStruct((1, 1, MODES, RADII), F32),
         ),
-        in_specs=[anywhere] * 3 + [scalar] * 4 + [vector] * 3 + [scalar],
+        in_specs=[anywhere] * 3 + [scalar] * 4 + [anywhere] * 3 + [scalar],
         out_specs=(vector, vector),
         scratch_shapes=[
             grid_of(7),
             grid_of(5),
             grid_of(5),
             grid_of(5),
+            pltpu.VMEM((1, PANELS), F32),
+            pltpu.VMEM((1, PANELS), I32),
+            pltpu.VMEM((1, PANELS), I32),
             pltpu.VMEM((4, 2, 7 * PLANES, RADII), F32),
             pltpu.VMEM((4, 2, 7 * PLANES, RADII), F32),
             pltpu.VMEM((4, 8, 128), F32),
             pltpu.VMEM((4, 8, 128), F32),
+            pltpu.VMEM((PLANES, COLS, 128), F32),
+            pltpu.VMEM((PLANES, COLS, 128), F32),
             pltpu.VMEM((ROWS, 128), BF16),
             pltpu.VMEM((128, ROWS), BF16),
             pltpu.VMEM((ROWS, 128), F32),
-            pltpu.VMEM((MEMBERS, 8, 128), F32),
-            pltpu.VMEM((MEMBERS, 8, 128), F32),
-            pltpu.VMEM((2, ROWS, 128), BF16),
-            pltpu.VMEM((2, 128, ROWS), BF16),
+            pltpu.VMEM((MEMBERS, 8, LANES), F32),
+            pltpu.VMEM((MEMBERS, 8, LANES), F32),
+            pltpu.VMEM((2, ROWS, LANES), BF16),
+            pltpu.VMEM((2, LANES, ROWS), BF16),
             pltpu.VMEM((MEMBERS, SLOTS, RADII), F32),
             pltpu.VMEM((MEMBERS, SLOTS, RADII), F32),
             pltpu.VMEM((GROUPS * WAVES, RADII), F32),
@@ -609,16 +690,17 @@
             pltpu.VMEM((GROUPS * WAVES, RADII), F32),
             pltpu.VMEM((MEMBERS, SLOTS, RADII), F32),
             pltpu.VMEM((MEMBERS, SLOTS, RADII), F32),
-            pltpu.SemaphoreType.DMA((3,)),
-            pltpu.SemaphoreType.DMA((5, 5)),
-            pltpu.SemaphoreType.DMA((5, 5)),
+            pltpu.SemaphoreType.DMA((6,)),
+            pltpu.SemaphoreType.DMA((5, 4)),
+            pltpu.SemaphoreType.DMA((5, 4)),
+            pltpu.SemaphoreType.DMA((2, 4)),
             pltpu.SemaphoreType.DMA((3,)),
             pltpu.SemaphoreType.DMA((3,)),
             pltpu.SemaphoreType.DMA((2, GROUPS - 1)),
             pltpu.SemaphoreType.DMA((2, GROUPS - 1)),
         ],
         compiler_params=pltpu.CompilerParams(
-            collective_id=0, has_side_effects=True, vmem_limit_bytes=32 << 20
+            collective_id=0, has_side_effects=True, vmem_limit_bytes=VMEM_GRANT
         ),
     )(
         state,

time: 106 us -> 84.8 us (0.80)
  the two profiles are of different devices: /device:TPU:1 before, /device:TPU:14 now
where the time goes in v2:
time: 84.8 us; the launch traced here: 84.5 us
  Pallas kernels  80.2 us (95%)
  local copies, waits for them, and re-layouts  3.05 us (4%)
  between operations  1.29 us (2%)
    pallas_call x1, Pallas kernels, local(): pl.pallas_call(kernel, out_shape=(jax.ShapeDtypeStruct((5, PLANES, COLS,...  80.2 us
    unnamed x1, local copies, waits for them, and re-layouts  1.72 us

profile of v2, /device:TPU:14, one launch (start us, length us, event | category | flops | bytes accessed | tf_op | source)
XLA Modules:
  0.0 84.5 jit_solution(18333868208833956712)
XLA Ops:
  1.3 80.2 %shard_map.122 = (f32[5,16,8,128]{3,2,1,0:T(8,128)}, f32[1,1,31,128]{3,2,1,0:T(8,128)}) custom-call(f32[5,16,8,128]{3,2,1,0:T(8,128)} %state.1, f32[16,8,128]{2,1,0:T(8,128)} %mean.1, f32[16,8,128]{2,1,0:T(8,128)} %sound.1, f32[5,5]{1,0:T(8,128)} %flux_a.1, f32[5,5]{1,0:T(8,128)} %flux_r.1, f32[5,5]{1,0:T(8,128)} %flux_t.1, s32[1,8]{1,0:T(1,128)} %pair.1, ...), custom_call_target="tpu_custom_call" | custom-call | tf_op jit(solution)/shard_map/pallas_call | solution.py:657
  81.5 1.3 %copy.13 = f32[1,1,31,128]{3,1,2,0:T(1,128)} copy(f32[1,1,31,128]{3,2,1,0:T(8,128)} %get-tuple-element.3) | data formatting | bytes 31744 | tf_op jit(solution)/shard_map/pallas_call | solution.py:657
  82.8 1.7 %copy.16 = f32[5,16,8,128]{3,2,1,0:T(8,128)} copy(f32[5,16,8,128]{3,2,1,0:T(8,128)} %get-tuple-element.6) | data formatting | bytes 655360

commit v3 on v2

--- a/solution.py
+++ b/solution.py
@@ -29,6 +29,7 @@
 KEEP = 1.0 - 6.0 * VISCOSITY * TIME_STEP
 SPREAD = VISCOSITY * TIME_STEP
 HALF = 0.5 * TIME_STEP
+FAR_FIRST = sorted(range(1, GROUPS), key=lambda k: abs(k - GROUPS // 2))
 UNROLL = 4
 VMEM_GRANT = 60 << 20
 MESH = pl.DeviceIdType.MESH
@@ -56,14 +57,14 @@
     state,
     mean,
     sound,
-    flux_a,
-    flux_r,
-    flux_t,
-    pair,
+    flux_a_in,
+    flux_r_in,
+    flux_t_in,
+    pair_in,
     weight_in,
     cell_in,
     owner_in,
-    count,
+    count_in,
     out,
     harm,
     q0,
@@ -73,10 +74,17 @@
     weight,
     cell,
     owner,
+    flux_a,
+    flux_r,
+    flux_t,
+    pair,
+    count,
     col_send,
     col_recv,
-    mir_send,
-    mir_recv,
+    tile,
+    near,
+    far,
+    far_near,
     rows0,
     turned,
     pick,
@@ -96,7 +104,8 @@
     load_sem,
     halo_send,
     halo_recv,
-    mirror_sems,
+    tile_send,
+    tile_recv,
     many_send,
     many_recv,
     few_send,
@@ -125,6 +134,11 @@
         pltpu.make_async_copy(weight_in, weight, load_sem.at[3]),
         pltpu.make_async_copy(cell_in, cell, load_sem.at[4]),
         pltpu.make_async_copy(owner_in, owner, load_sem.at[5]),
+        pltpu.make_async_copy(flux_a_in, flux_a, load_sem.at[6]),
+        pltpu.make_async_copy(flux_r_in, flux_r, load_sem.at[7]),
+        pltpu.make_async_copy(flux_t_in, flux_t, load_sem.at[8]),
+        pltpu.make_async_copy(pair_in, pair, load_sem.at[9]),
+        pltpu.make_async_copy(count_in, count, load_sem.at[10]),
     ]
     for load in lists + loads:
         load.start()
@@ -136,16 +150,22 @@
     def greet(to_sector, to_slab):
         pl.semaphore_signal(barrier, inc=1, device_id=(to_sector, to_slab), device_id_type=MESH)
 
+    behind_right = lax.rem(behind + 1, SECTORS)
+    behind_left = lax.rem(behind + SECTORS - 1, SECTORS)
     greet(right, slab)
     greet(left, slab)
+    greet(behind_right, slab)
+    greet(behind_left, slab)
 
     @pl.when(slab > 0)
     def _():
         greet(sector, slab - 1)
+        greet(behind, slab - 1)
 
     @pl.when(slab < SLABS - 1)
     def _():
         greet(sector, slab + 1)
+        greet(behind, slab + 1)
 
     for k in range(1, GROUPS):
         greet(twin(k), slab)
@@ -235,22 +255,28 @@
             columns.append(column)
         return columns
 
+    axial = matrix_columns(lambda f, g: flux_a[f, g] * HALF)
     radial = matrix_columns(lambda f, g: flux_r[f, g] * HALF)
-    radial_t = matrix_columns(lambda f, g: -flux_r[g, f] * HALF)
+    angular = matrix_columns(lambda f, g: flux_t[f, g] * (2.0 * HALF))
+    axial_t = matrix_columns(lambda f, g: flux_a[g, f] * HALF)
+    radial_t = matrix_columns(lambda f, g: flux_r[g, f] * HALF)
+    angular_t = matrix_columns(lambda f, g: flux_t[g, f] * (2.0 * HALF))
+    radial_back = [-column for column in radial_t]
 
     def met(columns, mirrored, speed):
-        total = columns[0] * mirrored[:1]
-        for g in range(1, 5):
-            total = total + columns[g] * mirrored[g : g + 1]
-        return jnp.where(sub < 5, mirrored * SPREAD + total * speed, 0.0)
+        return jnp.where(sub < 5, mirrored * SPREAD + mix(columns, mirrored) * speed, 0.0)
 
     @pl.when(slab == 0)
     def _():
+        for ref in (near, far_near):
+            ref[:, 3] = jnp.zeros((2, 8, 128), F32)
         for ref in (q0, q1, p0, p1):
             ref[:, 0] = jnp.zeros_like(ref[:, 0])
 
     @pl.when(slab == SLABS - 1)
     def _():
+        for ref in (near, far_near):
+            ref[:, 2] = jnp.zeros((2, 8, 128), F32)
         for ref in (q0, q1, p0, p1):
             ref[:, PLANES + 1] = jnp.zeros_like(ref[:, PLANES + 1])
 
@@ -299,24 +325,94 @@
         )
         return up, downward
 
-    def mirror_of(level):
+    def tile_copy(which, place, source, target, to):
         return pltpu.make_async_remote_copy(
-            src_ref=mir_send.at[level],
-            dst_ref=mir_recv.at[level],
-            send_sem=mirror_sems.at[0, level],
-            recv_sem=mirror_sems.at[1, level],
-            device_id=(behind, slab),
+            src_ref=source,
+            dst_ref=target,
+            send_sem=tile_send.at[which, place],
+            recv_sem=tile_recv.at[which, place],
+            device_id=to,
             device_id_type=MESH,
         )
 
-    def send_mirror(level):
-        mirror_of(level).start()
-        sent.append(lambda: mirror_of(level).wait_send())
-
-    def exchange(ref, level, phase, first, number, act):
+    slab_down, slab_up = lax.rem(slab + SLABS - 1, SLABS), lax.rem(slab + 1, SLABS)
+
+    def exchange_tiles(which, act):
+        inner = tile.at[which, pl.ds(0, 8)]
+        act(tile_copy(which, 8, tile.at[which], far.at[which], (behind, slab)), "both")
+        act(tile_copy(which, 4, inner, far_near.at[which, 0], (behind_left, slab)), "both")
+        act(tile_copy(which, 5, inner, far_near.at[which, 1], (behind_right, slab)), "both")
+        act(tile_copy(which, 0, inner, near.at[which, 0], (left, slab)), "both")
+        act(tile_copy(which, 1, inner, near.at[which, 1], (right, slab)), "both")
+        downward = (
+            tile_copy(which, 6, inner, far_near.at[which, 2], (behind, slab_down)),
+            tile_copy(which, 2, inner, near.at[which, 2], (sector, slab_down)),
+        )
+        upward = (
+            tile_copy(which, 7, inner, far_near.at[which, 3], (behind, slab_up)),
+            tile_copy(which, 3, inner, near.at[which, 3], (sector, slab_up)),
+        )
+
+        @pl.when(slab > 0)
+        def _():
+            for copy in downward:
+                act(copy, "send")
+            for copy in upward:
+                act(copy, "recv")
+
+        @pl.when(slab < SLABS - 1)
+        def _():
+            for copy in upward:
+                act(copy, "send")
+            for copy in downward:
+                act(copy, "recv")
+
+    def shifted(rows, beside):
+        from_right, from_left, from_up, from_down = beside
+        t_minus = jnp.where(ray % COLS == 0, pltpu.roll(from_left, 121, 1), pltpu.roll(rows, 1, 1))
+        t_plus = jnp.where(ray % COLS == 7, pltpu.roll(from_right, 7, 1), pltpu.roll(rows, 127, 1))
+        x_minus = jnp.where(ray < COLS, pltpu.roll(from_down, 8, 1), pltpu.roll(rows, 8, 1))
+        x_plus = jnp.where(ray >= 120, pltpu.roll(from_up, 120, 1), pltpu.roll(rows, 120, 1))
+        return x_minus, x_plus, t_minus, t_plus
+
+    def mix(columns, fields):
+        total = columns[0] * fields[:1]
+        for g in range(1, 5):
+            total = total + columns[g] * fields[g : g + 1]
+        return total
+
+    def forward_inner(rows, following, beside, speed, flow):
+        x_minus, x_plus, t_minus, t_plus = shifted(rows, beside)
+        dx = x_plus - x_minus
+        mixed = mix(axial, dx) + mix(angular, t_plus - t_minus)
+        around = x_plus + x_minus + t_plus + t_minus
+        if following is not None:
+            mixed, around = mixed + mix(radial, following), around + following
+        result = rows * KEEP + around * SPREAD - (flow * HALF) * dx - speed * mixed
+        return jnp.where(sub < 5, result, 0.0)
+
+    def adjoint_inner(rows, following, beside, coefs, speed_next):
+        x_minus, x_plus, t_minus, t_plus = shifted(rows, beside)
+        k_x_minus, k_x_plus, k_t_minus, k_t_plus = coefs
+        result = mix(axial_t, x_plus * k_x_plus[5:6] - x_minus * k_x_minus[5:6])
+        result = result + mix(angular_t, t_plus * k_t_plus[5:6] - t_minus * k_t_minus[5:6])
+        result = result + (x_plus * k_x_plus[6:7] - x_minus * k_x_minus[6:7]) * HALF
+        around = x_plus + x_minus + t_plus + t_minus
+        if following is not None:
+            result, around = result + mix(radial_t, following * speed_next), around + following
+        result = result + rows * KEEP + around * SPREAD
+        return jnp.where(sub < 5, result, 0.0)
+
+    def stack(which):
+        return jnp.concatenate([far[which][:8], far_near[which, 2], far_near[which, 3]], axis=0)
+
+    def exchange(ref, level, phase, first, number, act, planes_first=None):
         for copy in columns_of(ref, level, phase, first, number):
             act(copy, "both")
-        up, downward = planes_of(ref, phase, first, number)
+        if planes_first is None:
+            up, downward = planes_of(ref, phase, first, number)
+        else:
+            up, downward = planes_of(ref, phase, planes_first, first + number - planes_first)
 
         @pl.when(slab < SLABS - 1)
         def _():
@@ -340,81 +436,76 @@
         if part_of != "recv":
             copy.wait_send()
 
+    wanted = jnp.where(row[:16] < 8, 2 * row[:16], 2 * (row[:16] - 8) + 1)
+    chosen = jnp.where(lane[:16] == wanted, 1.0, 0.0).astype(BF16)
+
     def pack_inner(i, fields):
         here = jnp.zeros((8, 128), F32)
         for f, value in enumerate(fields):
-            here = jnp.where(ray == f, value if f == 0 else pltpu.roll(value, f, 1), here)
+            here = jnp.where(ray // 2 == f, value if f == 0 else pltpu.roll(value, 2 * f, 1), here)
         rows0[i] = here
 
     def packed():
-        return rows0[...].reshape(128, 128).T[:8]
-
-    def unpack(fields):
-        wide = jnp.concatenate([fields, jnp.zeros((120, 128), F32)], axis=0)
+        high, low = split(rows0[...].reshape(128, 128))
+        both = dot_nt(chosen, high) + dot_nt(chosen, low)
+        return both[:8], both[8:]
+
+    def patch(ref, skip, inner, following, fields):
+        wide = jnp.concatenate([inner, following, jnp.zeros((112, 128), F32)], axis=0)
         turned[...] = wide.T.reshape(PLANES, COLS, 128)
 
-    def lane_zero(inner, f):
-        return inner if f == 0 else pltpu.roll(inner, 128 - f, 1)
-
-    def add_inner(ref):
         def step(i, carry):
-            inner = turned[i]
-            for f in range(5):
-                ref[f, i + 1] += jnp.where(ray == 0, lane_zero(inner, f), 0.0)
+            here = turned[i]
+            for f in fields:
+                zero = here if f == 0 else pltpu.roll(here, 128 - f, 1)
+                one = pltpu.roll(here, 121 - f, 1)
+                ref[f, i + skip] += jnp.where(ray == 0, zero, jnp.where(ray == 1, one, 0.0))
             return carry
 
         lax.fori_loop(0, PLANES, step, 0, unroll=4)
 
-    def beside(value, level, f, i, inner):
+    def beside(value, level, f, i):
         before = jnp.broadcast_to(col_recv[level, 1, pl.ds(f * PLANES + i, 1), :], (8, 128))
         after = jnp.broadcast_to(col_recv[level, 0, pl.ds(f * PLANES + i, 1), :], (8, 128))
         t_minus = jnp.where(sub == 0, before, pltpu.roll(value, 1, 0))
         t_plus = jnp.where(sub == COLS - 1, after, pltpu.roll(value, COLS - 1, 0))
-        core = 0.0 if inner is None else lane_zero(inner, f)
-        r_minus = jnp.where(ray == 0, core, pltpu.roll(value, 1, 1))
+        r_minus = jnp.where(ray == 0, 0.0, pltpu.roll(value, 1, 1))
         r_plus = jnp.where(ray == RADII - 1, 0.0, pltpu.roll(value, RADII - 1, 1))
         return t_minus, t_plus, r_minus, r_plus
 
     inverse = 1.0 / (ray.astype(F32) + 0.5)
 
-    def forward_plane(src, level, dst, mirrored, i):
+    def forward_plane(src, level, dst, i):
         u, c = q0[5, i + 1] * HALF, q0[6, i + 1] * HALF
-        inner = turned[i] if mirrored else None
         values, dx, dr, dt, around = [], [], [], [], []
         for f in range(5):
             value, x_minus, x_plus = src[f, i + 1], src[f, i], src[f, i + 2]
-            t_minus, t_plus, r_minus, r_plus = beside(value, level, f, i, inner)
+            t_minus, t_plus, r_minus, r_plus = beside(value, level, f, i)
             values.append(value)
             dx.append(x_plus - x_minus)
             dr.append(r_plus - r_minus)
             dt.append((t_plus - t_minus) * inverse)
             around.append((x_plus + x_minus) + (t_plus + t_minus) + (r_plus + r_minus))
-        results = []
         for f in range(5):
             mixed = flux_a[f, 0] * dx[0] + flux_r[f, 0] * dr[0] + flux_t[f, 0] * dt[0]
             for g in range(1, 5):
                 mixed = mixed + flux_a[f, g] * dx[g] + flux_r[f, g] * dr[g] + flux_t[f, g] * dt[g]
-            result = values[f] * KEEP + around[f] * SPREAD - u * dx[f] - c * mixed
-            dst[f, i + 1] = result
-            results.append(result)
-        pack_inner(i, results)
-
-    def adjoint_plane(src, level, store, mirrored, i):
+            dst[f, i + 1] = values[f] * KEEP + around[f] * SPREAD - u * dx[f] - c * mixed
+
+    def adjoint_plane(src, level, store, i):
         u_minus, u_plus = q0[5, i] * HALF, q0[5, i + 2] * HALF
         c = q0[6, i + 1] * HALF
         c_minus, c_plus = q0[6, i] * HALF, q0[6, i + 2] * HALF
         before = jnp.broadcast_to(col_recv[0, 1, pl.ds(6 * PLANES + i, 1), :], (8, 128)) * HALF
         after = jnp.broadcast_to(col_recv[0, 0, pl.ds(6 * PLANES + i, 1), :], (8, 128)) * HALF
-        inner = turned[i] if mirrored else None
         c_t_minus = jnp.where(sub == 0, before, pltpu.roll(c, 1, 0)) * inverse
         c_t_plus = jnp.where(sub == COLS - 1, after, pltpu.roll(c, COLS - 1, 0)) * inverse
-        core = lane_zero(inner, 5) * HALF if mirrored else 0.0
-        c_r_minus = jnp.where(ray == 0, core, pltpu.roll(c, 1, 1))
+        c_r_minus = pltpu.roll(c, 1, 1)
         c_r_plus = pltpu.roll(c, RADII - 1, 1)
         carried, dx, dr, dt = [], [], [], []
         for f in range(5):
             value, x_minus, x_plus = src[f, i + 1], src[f, i], src[f, i + 2]
-            t_minus, t_plus, r_minus, r_plus = beside(value, level, f, i, inner)
+            t_minus, t_plus, r_minus, r_plus = beside(value, level, f, i)
             dx.append(c_plus * x_plus - c_minus * x_minus)
             dr.append(c_r_plus * r_plus - c_r_minus * r_minus)
             dt.append(c_t_plus * t_plus - c_t_minus * t_minus)
@@ -422,15 +513,11 @@
             carried.append(
                 value * KEEP + around * SPREAD + (u_plus * x_plus - u_minus * x_minus)
             )
-        results = []
         for f in range(5):
             result = carried[f]
             for g in range(5):
                 result = result + flux_a[g, f] * dx[g] + flux_r[g, f] * dr[g] + flux_t[g, f] * dt[g]
             store(f, i, result)
-            results.append(result)
-        if not mirrored:
-            pack_inner(i, results)
 
     def planes(body):
         def step(i, carry):
@@ -441,17 +528,20 @@
 
     for load in loads:
         load.wait()
-    pack_columns(q0, 0, range(7))
-    planes(lambda i: pack_inner(i, [q0[f, i + 1] for f in (0, 1, 2, 3, 4, 6)]))
-    first_rows = jnp.where(sub == 6, pairs.astype(F32), packed())
-    mir_send[0] = first_rows
+    pack_columns(q0, 0, (0, 1, 2, 3, 4, 6))
+    planes(lambda i: pack_inner(i, [q0[f, i + 1] for f in (0, 1, 2, 3, 4, 6, 5)]))
+    first_rows, first_next = packed()
+    first_rows = jnp.where(sub == 7, pairs.astype(F32), first_rows)
+    tile[0, :8] = first_rows
+    tile[0, 8:] = first_next
     pl.semaphore_wait(
         barrier,
-        MEMBERS - 1 + GROUPS - 1 + 2 + jnp.where(slab > 0, 1, 0) + jnp.where(slab < SLABS - 1, 1, 0),
+        MEMBERS - 1 + GROUPS - 1 + 4 + jnp.where(slab > 0, 2, 0) + jnp.where(slab < SLABS - 1, 2, 0),
     )
-    send_mirror(0)
-    exchange(q0, 0, 0, 0, 7, start)
-    sent.append(lambda: exchange(q0, 0, 0, 0, 7, leave))
+    exchange_tiles(0, start)
+    sent.append(lambda: exchange_tiles(0, leave))
+    exchange(q0, 0, 0, 0, 5, start)
+    sent.append(lambda: exchange(q0, 0, 0, 0, 5, leave))
 
     def to_mate(source, target, which):
         def copy_of(r):
@@ -484,7 +574,8 @@
             copy_of(r).start()
             return carry
 
-        lax.fori_loop(1, MEMBERS, step, 0)
+        lax.fori_loop(4, MEMBERS, step, 0)
+        lax.fori_loop(1, 4, step, 0)
 
     def all_of(source, target, which):
         rest = pl.ds(1, MEMBERS - 1)
@@ -497,30 +588,47 @@
             device_id_type=MESH,
         )
 
-    start_all(to_mate(wave_out, wave_in, 0))
-    sent.append(lambda: all_of(wave_out, wave_in, 0).wait_send())
     wave_in[0] = wave_out[0]
-    exchange(q0, 0, 0, 0, 7, arrive)
-    planes(functools.partial(forward_plane, q0, 0, q1, False))
-    mir_send[1] = packed()
-    send_mirror(1)
-    mirror_of(0).wait_recv()
-    theirs = mir_recv[0]
-    mirrored = across_axis(theirs, cross)
-    core_speed = mirrored[5:6]
-    unpack(met(radial, mirrored * parity, first_rows[5:6]))
-    add_inner(q1)
+    exchange(q0, 0, 0, 0, 5, arrive)
+    planes(functools.partial(forward_plane, q0, 0, q1))
     pack_columns(q1, 1, range(5))
     exchange(q1, 1, 1, 0, 5, start)
     sent.append(lambda: exchange(q1, 1, 1, 0, 5, leave))
-    cross_back = crossing(theirs[6:7].astype(I32))
+    start_all(to_mate(wave_out, wave_in, 0))
+    sent.append(lambda: all_of(wave_out, wave_in, 0).wait_send())
+    exchange(q1, 1, 1, 0, 5, arrive)
+    planes(functools.partial(forward_plane, q1, 1, p0))
+    exchange_tiles(0, arrive)
+    theirs, theirs_next = far[0][:8], far[0][8:]
+    by_us = [near[0, k] for k in range(4)]
+    by_them = [far_near[0, k] for k in range(4)]
+    cross_right = crossing(by_us[0][7:8].astype(I32))
+    cross_left = crossing(by_us[1][7:8].astype(I32))
+    cross_back = crossing(theirs[7:8].astype(I32))
+
+    def opposite_values(which):
+        three = across_axis(stack(which), cross)
+        return [
+            three[:8],
+            across_axis(far_near[which, 0], cross_right),
+            across_axis(far_near[which, 1], cross_left),
+            three[8:16],
+            three[16:],
+        ]
+
+    met_values = opposite_values(0)
+    met_speeds = [values[5:6] for values in met_values]
+    speed, speed_next, flow = first_rows[5:6], first_next[5:6], first_rows[6:7]
+    speeds = [speed] + [values[5:6] for values in by_us]
+    added = [met(radial, values * parity, at) for values, at in zip(met_values, speeds)]
     there = across_axis(first_rows, cross_back)
-    core_speed_there = there[5:6]
-    addition = met(radial, there * parity, theirs[5:6])
-    mirror_of(1).wait_recv()
-    unpack(across_axis(mir_recv[1] + addition, cross) * parity)
-    exchange(q1, 1, 1, 0, 5, arrive)
-    planes(functools.partial(forward_plane, q1, 1, p0, True))
+    met_speed_there = there[5:6]
+    theirs_after = forward_inner(theirs, theirs_next, by_them, theirs[5:6], theirs[6:7])
+    theirs_after = theirs_after + met(radial, there * parity, theirs[5:6])
+    mirrored = across_axis(theirs_after, cross) * parity
+    inner = forward_inner(added[0], None, added[1:], speed, flow) + met(radial, mirrored, speed)
+    following = met(radial, added[0], speed_next)
+    patch(p0, 1, inner, following, (4,))
 
     pressure = p0[4, 1 : PLANES + 1].reshape(PLANES * COLS, RADII)
     high, low = split(pressure)
@@ -529,10 +637,9 @@
     start_all(to_mate(lines_out, lines_in, 1))
     sent.append(lambda: all_of(lines_out, lines_in, 1).wait_send())
     lines_in[0] = lines_out[0]
-    forward_rows = packed()
-    pack_columns(p0, 2, range(4))
-    exchange(p0, 2, 2, 0, 4, start)
-    sent.append(lambda: exchange(p0, 2, 2, 0, 4, leave))
+    patch(p0, 1, inner, following, range(4))
+    planes(lambda i: pack_inner(i, [p0[f, i + 1] for f in range(4)]))
+    forward_rows, forward_next = packed()
     all_of(wave_out, wave_in, 0).wait_recv()
     given = wave_in[...]
     sub3, ray3 = iota((MEMBERS, 8, LANES), 1), iota((MEMBERS, 8, LANES), 2)
@@ -569,18 +676,23 @@
             device_id_type=MESH,
         )
 
-    for k in range(1, GROUPS):
+    for k in FAR_FIRST:
         to_twin(k).start()
         sent.append(lambda k=k: to_twin(k).wait_send())
+    pack_columns(p0, 2, range(4))
+    exchange(p0, 2, 2, 0, 4, start)
+    sent.append(lambda: exchange(p0, 2, 2, 0, 4, leave))
+    exchange(q0, 0, 5, 6, 1, start, 5)
+    sent.append(lambda: exchange(q0, 0, 5, 6, 1, leave, 5))
     mine = part[own_rows, :]
     for k in range(1, GROUPS):
         to_twin(k).wait_recv()
         mine = mine + part_in[k - 1]
     whole[own_rows, :] = mine
-    for k in range(1, GROUPS):
+    for k in FAR_FIRST:
         from_owner(k).start()
         sent.append(lambda k=k: from_owner(k).wait_send())
-    harm[0, 0] = mine[:MODES]
+    harm[:, 0] = mine[:MODES]
     for k in range(1, GROUPS):
         from_owner(k).wait_recv()
 
@@ -598,12 +710,17 @@
     p0[4, 1 : PLANES + 1] = p0[4, 1 : PLANES + 1] + impulse
 
     pressure = p0[4, 1 : PLANES + 1].reshape(PLANES * COLS, RADII)
-    start_rows = jnp.where(sub == 4, pressure.T[:1], forward_rows)
-    mir_send[2] = start_rows
-    send_mirror(2)
+    pressure = pressure.T
+    start_rows = jnp.where(sub == 4, pressure[:1], forward_rows)
+    start_next = jnp.where(sub == 4, pressure[1:2], forward_next)
+    tile[1, :8] = start_rows
+    tile[1, 8:] = start_next
+    exchange_tiles(1, start)
+    sent.append(lambda: exchange_tiles(1, leave))
     pack_columns(p0, 2, (4,))
     exchange(p0, 2, 3, 4, 1, start)
     sent.append(lambda: exchange(p0, 2, 3, 4, 1, leave))
+    exchange(q0, 0, 5, 6, 1, arrive, 5)
     exchange(p0, 2, 3, 4, 1, arrive)
 
     def store_p1(f, i, value):
@@ -612,23 +729,32 @@
     def store_out(f, i, value):
         out[f, i] = value
 
-    planes(functools.partial(adjoint_plane, p0, 2, store_p1, False))
-    mir_send[3] = packed()
-    send_mirror(3)
-    there = across_axis(start_rows, cross_back) * parity
-    addition = met(radial_t, there, core_speed_there)
-    mirror_of(2).wait_recv()
-    mirrored = across_axis(mir_recv[2], cross) * parity
-    unpack(met(radial_t, mirrored, core_speed))
-    add_inner(p1)
+    planes(functools.partial(adjoint_plane, p0, 2, store_p1))
     pack_columns(p1, 3, range(5))
     exchange(p1, 3, 4, 0, 5, start)
     sent.append(lambda: exchange(p1, 3, 4, 0, 5, leave))
-    mirror_of(3).wait_recv()
-    mirrored = across_axis(mir_recv[3] + addition, cross) * parity
-    unpack(jnp.where(sub == 5, core_speed, mirrored))
     exchange(p1, 3, 4, 0, 5, arrive)
-    planes(functools.partial(adjoint_plane, p1, 3, store_out, True))
+    planes(functools.partial(adjoint_plane, p1, 3, store_out))
+    exchange_tiles(1, arrive)
+    coefs = shifted(first_rows, by_us)
+    added = [
+        met(radial_back, values * parity, at) for values, at in zip(opposite_values(1), met_speeds)
+    ]
+    theirs, theirs_follow = far[1][:8], far[1][8:]
+    theirs_after = adjoint_inner(
+        theirs,
+        theirs_follow,
+        [far_near[1, k] for k in range(4)],
+        shifted(far[0][:8], by_them),
+        theirs_next[5:6],
+    )
+    there = across_axis(start_rows, cross_back) * parity
+    theirs_after = theirs_after + met(radial_back, there, met_speed_there)
+    mirrored = across_axis(theirs_after, cross) * parity
+    inner = adjoint_inner(added[0], None, added[1:], coefs, None)
+    inner = inner + met(radial_back, mirrored, met_speeds[0])
+    following = met(radial_back, added[0], speed)
+    patch(out, 0, inner, following, range(5))
 
     for wait in sent:
         wait()
@@ -647,20 +773,19 @@
     panel_owner,
     panel_count,
 ):
-    anywhere = pl.BlockSpec(memory_space=pl.ANY)
-    scalar = pl.BlockSpec(memory_space=pltpu.SMEM)
+    outside = pl.BlockSpec(memory_space=pltpu.HBM)
     vector = pl.BlockSpec(memory_space=pltpu.VMEM)
 
     def grid_of(fields):
         return pltpu.VMEM((fields, PLANES + 2, COLS, RADII), F32)
 
-    return pl.pallas_call(
+    fields, rows = pl.pallas_call(
         kernel,
         out_shape=(
             jax.ShapeDtypeStruct((5, PLANES, COLS, RADII), F32),
-            jax.ShapeDtypeStruct((1, 1, MODES, RADII), F32),
+            jax.ShapeDtypeStruct((MODES, 1, RADII), F32),
         ),
-        in_specs=[anywhere] * 3 + [scalar] * 4 + [anywhere] * 3 + [scalar],
+        in_specs=[outside] * 11,
         out_specs=(vector, vector),
         scratch_shapes=[
             grid_of(7),
@@ -670,10 +795,17 @@
             pltpu.VMEM((1, PANELS), F32),
             pltpu.VMEM((1, PANELS), I32),
             pltpu.VMEM((1, PANELS), I32),
+            pltpu.SMEM((5, 5), F32),
+            pltpu.SMEM((5, 5), F32),
+            pltpu.SMEM((5, 5), F32),
+            pltpu.SMEM((1, COLS), I32),
+            pltpu.SMEM((1, 1), I32),
             pltpu.VMEM((4, 2, 7 * PLANES, RADII), F32),
             pltpu.VMEM((4, 2, 7 * PLANES, RADII), F32),
-            pltpu.VMEM((4, 8, 128), F32),
-            pltpu.VMEM((4, 8, 128), F32),
+            pltpu.VMEM((2, 16, 128), F32),
+            pltpu.VMEM((2, 4, 8, 128), F32),
+            pltpu.VMEM((2, 16, 128), F32),
+            pltpu.VMEM((2, 4, 8, 128), F32),
             pltpu.VMEM((PLANES, COLS, 128), F32),
             pltpu.VMEM((PLANES, COLS, 128), F32),
             pltpu.VMEM((ROWS, 128), BF16),
@@ -690,10 +822,11 @@
             pltpu.VMEM((GROUPS * WAVES, RADII), F32),
             pltpu.VMEM((MEMBERS, SLOTS, RADII), F32),
             pltpu.VMEM((MEMBERS, SLOTS, RADII), F32),
-            pltpu.SemaphoreType.DMA((6,)),
-            pltpu.SemaphoreType.DMA((5, 4)),
-            pltpu.SemaphoreType.DMA((5, 4)),
-            pltpu.SemaphoreType.DMA((2, 4)),
+            pltpu.SemaphoreType.DMA((11,)),
+            pltpu.SemaphoreType.DMA((6, 4)),
+            pltpu.SemaphoreType.DMA((6, 4)),
+            pltpu.SemaphoreType.DMA((2, 9)),
+            pltpu.SemaphoreType.DMA((2, 9)),
             pltpu.SemaphoreType.DMA((3,)),
             pltpu.SemaphoreType.DMA((3,)),
             pltpu.SemaphoreType.DMA((2, GROUPS - 1)),
@@ -715,6 +848,7 @@
         panel_owner.reshape(1, PANELS),
         panel_count,
     )
+    return fields, rows.reshape(1, 1, MODES, RADII)
 
 
 def solution(mesh):

time: 84.8 us -> 77.3 us (0.912)
  the two profiles are of different devices: /device:TPU:14 before, /device:TPU:1 now
where the time goes in v3:
time: 77.3 us; the launch traced here: 77.1 us
  Pallas kernels  73.5 us (95%)
  local copies, waits for them, and re-layouts  2.33 us (3%)
  between operations  1.3 us (2%)
    pallas_call x1, Pallas kernels, local(): pl.pallas_call(kernel, out_shape=(jax.ShapeDtypeStruct((5, PLANES, COLS,...  73.5 us
    unnamed x4, local copies, waits for them, and re-layouts  2.33 us

profile of v3, /device:TPU:1, one launch (start us, length us, event | category | flops | bytes accessed | tf_op | source)
XLA Modules:
  0.0 77.1 jit_solution(14637968157744037042)
XLA Ops:
  1.3 73.5 %shard_map.122 = (f32[5,16,8,128]{3,2,1,0:T(8,128)}, f32[31,1,128]{2,1,0:T(1,128)}) custom-call(f32[5,16,8,128]{3,2,1,0:T(8,128)} %state.1, f32[16,8,128]{2,1,0:T(8,128)} %mean.1, f32[16,8,128]{2,1,0:T(8,128)} %sound.1, f32[5,5]{1,0:T(8,128)} %flux_a_in.1, f32[5,5]{1,0:T(8,128)} %flux_r_in.1, f32[5,5]{1,0:T(8,128)} %flux_t_in.1, s32[1,8]{1,0:T(1,128)} %pair_in.1, ...), custom_call_target="tpu_custom_call" | custom-call | tf_op jit(solution)/shard_map/pallas_call | solution.py:782
  74.8 0.0 copy-start
  74.8 1.7 %copy.17 = f32[5,16,8,128]{3,2,1,0:T(8,128)} copy(f32[5,16,8,128]{3,2,1,0:T(8,128)} %get-tuple-element.10) | data formatting | bytes 655360
  76.5 0.0 copy-done
  76.5 0.6 copy.18
Async XLA Ops:
  74.8 1.7 %copy-start = (f32[31,1,128]{2,1,0:T(1,128)S(1)}, f32[31,1,128]{2,1,0:T(1,128)}, u32[]{:S(2)}) copy-start(f32[31,1,128]{2,1,0:T(1,128)} %get-tuple-element.5) | copy-start | bytes 47620

commit v4 on v3

--- a/solution.py
+++ b/solution.py
@@ -29,7 +29,9 @@
 KEEP = 1.0 - 6.0 * VISCOSITY * TIME_STEP
 SPREAD = VISCOSITY * TIME_STEP
 HALF = 0.5 * TIME_STEP
-FAR_FIRST = sorted(range(1, GROUPS), key=lambda k: abs(k - GROUPS // 2))
+ORDER = (4, 3, 5, 2, 6, 1, 7, 0)
+HALVES = (ORDER[: GROUPS // 2], ORDER[GROUPS // 2 :])
+PART = SLOTS // 2
 UNROLL = 4
 VMEM_GRANT = 60 << 20
 MESH = pl.DeviceIdType.MESH
@@ -125,6 +127,39 @@
     def twin(k):
         return lax.rem(group + k, GROUPS) * MEMBERS + member
 
+    sent = []
+
+    barrier = pltpu.get_barrier_semaphore()
+
+    def greet(to_sector, to_slab):
+        pl.semaphore_signal(barrier, inc=1, device_id=(to_sector, to_slab), device_id_type=MESH)
+
+    behind_right = lax.rem(behind + 1, SECTORS)
+    behind_left = lax.rem(behind + SECTORS - 1, SECTORS)
+    greet(right, slab)
+    greet(left, slab)
+    greet(behind_right, slab)
+    greet(behind_left, slab)
+
+    @pl.when(slab > 0)
+    def _():
+        greet(sector, slab - 1)
+        greet(behind, slab - 1)
+
+    @pl.when(slab < SLABS - 1)
+    def _():
+        greet(sector, slab + 1)
+        greet(behind, slab + 1)
+
+    for k in range(1, GROUPS):
+        greet(twin(k), slab)
+
+    def greet_mate(r, carry):
+        greet(mate(r), slab)
+        return carry
+
+    lax.fori_loop(1, MEMBERS, greet_mate, 0)
+
     loads = [
         pltpu.make_async_copy(state, q0.at[pl.ds(0, 5), pl.ds(1, PLANES)], load_sem.at[0]),
         pltpu.make_async_copy(mean, q0.at[5, pl.ds(1, PLANES)], load_sem.at[1]),
@@ -143,38 +178,6 @@
     for load in lists + loads:
         load.start()
 
-    sent = []
-
-    barrier = pltpu.get_barrier_semaphore()
-
-    def greet(to_sector, to_slab):
-        pl.semaphore_signal(barrier, inc=1, device_id=(to_sector, to_slab), device_id_type=MESH)
-
-    behind_right = lax.rem(behind + 1, SECTORS)
-    behind_left = lax.rem(behind + SECTORS - 1, SECTORS)
-    greet(right, slab)
-    greet(left, slab)
-    greet(behind_right, slab)
-    greet(behind_left, slab)
-
-    @pl.when(slab > 0)
-    def _():
-        greet(sector, slab - 1)
-        greet(behind, slab - 1)
-
-    @pl.when(slab < SLABS - 1)
-    def _():
-        greet(sector, slab + 1)
-        greet(behind, slab + 1)
-
-    for k in range(1, GROUPS):
-        greet(twin(k), slab)
-
-    def greet_mate(r, carry):
-        greet(mate(r), slab)
-        return carry
-
-    lax.fori_loop(1, MEMBERS, greet_mate, 0)
 
     row = iota((128, 128), 0)
     lane = iota((128, 128), 1)
@@ -199,7 +202,12 @@
         at = slice(q * 128, (q + 1) * 128)
         name = owners[:, at]
         relative = (name + MEMBERS - member) % MEMBERS
-        slot = relative * SLOTS + (name // MEMBERS) * CAP + rank
+        ahead = (name // MEMBERS + GROUPS - group) % GROUPS
+        position = jnp.zeros((1, 128), I32)
+        for at_position, k in enumerate(ORDER):
+            position = jnp.where(ahead == k, at_position, position)
+        half = position // (GROUPS // 2)
+        slot = (half * MEMBERS + relative) * PART + (position % (GROUPS // 2)) * CAP + rank
         place = iota((1, 128), 1) + q * 128
         slot = jnp.where(place < live, slot, -1)
         slot_pieces.append(jnp.where(tall == slot, 1.0, 0.0).astype(BF16))
@@ -222,11 +230,10 @@
     table_high, table_low = split(table)
     waves = dot(picked, table_high) + dot(picked, table_low)
     tall, tall_lane = iota((ROWS, LANES), 0), iota((ROWS, LANES), 1)
-    waves = jnp.where((tall % SLOTS) // CAP == tall_lane // WAVES, waves, 0.0)
-    waves = waves.reshape(MEMBERS, SLOTS, LANES)
-    halves = waves[:, :8]
-    for h in range(1, SLOTS // 8):
-        halves = halves + waves[:, h * 8 : (h + 1) * 8]
+    position = (tall % PART) // CAP + (tall // (MEMBERS * PART)) * (GROUPS // 2)
+    waves = jnp.where(position == tall_lane // WAVES, waves, 0.0)
+    waves = waves.reshape(2, MEMBERS, PART, LANES)
+    halves = (waves[0, :, :8] + waves[0, :, 8:]) + (waves[1, :, :8] + waves[1, :, 8:])
     wave_out[...] = halves + jnp.concatenate([halves[:, 4:], halves[:, :4]], axis=1)
 
     sub = iota((8, 128), 0)
@@ -543,31 +550,21 @@
     exchange(q0, 0, 0, 0, 5, start)
     sent.append(lambda: exchange(q0, 0, 0, 0, 5, leave))
 
+    def mate_copy(source, target, which, r, to):
+        return pltpu.make_async_remote_copy(
+            src_ref=source.at[r],
+            dst_ref=target.at[r],
+            send_sem=many_send.at[which],
+            recv_sem=many_recv.at[which],
+            device_id=(to, slab),
+            device_id_type=MESH,
+        )
+
     def to_mate(source, target, which):
-        def copy_of(r):
-            return pltpu.make_async_remote_copy(
-                src_ref=source.at[r],
-                dst_ref=target.at[r],
-                send_sem=many_send.at[which],
-                recv_sem=many_recv.at[which],
-                device_id=(mate(r), slab),
-                device_id_type=MESH,
-            )
-
-        return copy_of
+        return lambda r: mate_copy(source, target, which, r, mate(r))
 
     def back_mate(source, target, which):
-        def copy_of(r):
-            return pltpu.make_async_remote_copy(
-                src_ref=source.at[r],
-                dst_ref=target.at[r],
-                send_sem=many_send.at[which],
-                recv_sem=many_recv.at[which],
-                device_id=(mate(MEMBERS - r), slab),
-                device_id_type=MESH,
-            )
-
-        return copy_of
+        return lambda r: mate_copy(source, target, which, r, mate(MEMBERS - r))
 
     def start_all(copy_of):
         def step(r, carry):
@@ -633,30 +630,32 @@
     pressure = p0[4, 1 : PLANES + 1].reshape(PLANES * COLS, RADII)
     high, low = split(pressure)
     lines = (dot(pick[...], high) + dot(pick[...], low)) * factor[...]
-    lines_out[...] = lines.reshape(MEMBERS, SLOTS, RADII)
-    start_all(to_mate(lines_out, lines_in, 1))
-    sent.append(lambda: all_of(lines_out, lines_in, 1).wait_send())
-    lines_in[0] = lines_out[0]
+    lines_out[...] = lines.reshape(2, MEMBERS, PART, RADII)
+    for h in range(2):
+        start_all(to_mate(lines_out.at[h], lines_in.at[h], 1 + h))
+        sent.append(lambda h=h: all_of(lines_out.at[h], lines_in.at[h], 1 + h).wait_send())
+        lines_in[h, 0] = lines_out[h, 0]
     patch(p0, 1, inner, following, range(4))
     planes(lambda i: pack_inner(i, [p0[f, i + 1] for f in range(4)]))
     forward_rows, forward_next = packed()
+    pack_columns(p0, 2, range(4))
     all_of(wave_out, wave_in, 0).wait_recv()
     given = wave_in[...]
-    sub3, ray3 = iota((MEMBERS, 8, LANES), 1), iota((MEMBERS, 8, LANES), 2)
-    quarters = []
-    for h in range(SLOTS // 8):
-        quarters.append(jnp.where(sub3 // CAP + 2 * h == ray3 // WAVES, given, 0.0))
-    encoder = jnp.concatenate(quarters, axis=1).reshape(ROWS, LANES)
-    enc[0], enc[1] = split(encoder)
-    enc_t[0], enc_t[1] = split(encoder.T)
-
-    all_of(lines_out, lines_in, 1).wait_recv()
-    high, low = split(lines_in[...].reshape(ROWS, RADII))
-    part[...] = dot(enc_t[0], high) + (dot(enc_t[0], low) + dot(enc_t[1], high))
+    sub3, ray3 = iota((MEMBERS, 8, 128), 1), iota((MEMBERS, 8, 128), 2)
+    for h in range(2):
+        some = given[:, :, h * 128 : (h + 1) * 128]
+        first = jnp.where(sub3 // CAP == ray3 // WAVES, some, 0.0)
+        second = jnp.where(sub3 // CAP + 2 == ray3 // WAVES, some, 0.0)
+        encoder = jnp.concatenate([first, second], axis=1).reshape(MEMBERS * PART, 128)
+        enc[h, 0], enc[h, 1] = split(encoder)
+        enc_t[h, 0], enc_t[h, 1] = split(encoder.T)
+
+    def rows_of(k):
+        return pl.ds(ORDER.index(k % GROUPS) * WAVES, WAVES)
 
     def to_twin(k):
         return pltpu.make_async_remote_copy(
-            src_ref=part.at[pl.ds(pl.multiple_of(lax.rem(group + k, GROUPS) * WAVES, WAVES), WAVES)],
+            src_ref=part.at[rows_of(k)],
             dst_ref=part_in.at[k - 1],
             send_sem=few_send.at[0, k - 1],
             recv_sem=few_recv.at[0, k - 1],
@@ -664,46 +663,53 @@
             device_id_type=MESH,
         )
 
-    own_rows = pl.ds(pl.multiple_of(group * WAVES, WAVES), WAVES)
-
     def from_owner(k):
         return pltpu.make_async_remote_copy(
-            src_ref=whole.at[own_rows],
-            dst_ref=whole.at[own_rows],
+            src_ref=whole.at[rows_of(0)],
+            dst_ref=whole.at[rows_of(GROUPS - k)],
             send_sem=few_send.at[1, k - 1],
             recv_sem=few_recv.at[1, k - 1],
             device_id=(twin(k), slab),
             device_id_type=MESH,
         )
 
-    for k in FAR_FIRST:
-        to_twin(k).start()
-        sent.append(lambda k=k: to_twin(k).wait_send())
-    pack_columns(p0, 2, range(4))
+    for h in range(2):
+        all_of(lines_out.at[h], lines_in.at[h], 1 + h).wait_recv()
+        high, low = split(lines_in[h].reshape(MEMBERS * PART, RADII))
+        part[h * 128 : (h + 1) * 128] = dot(enc_t[h, 0], high) + (
+            dot(enc_t[h, 0], low) + dot(enc_t[h, 1], high)
+        )
+        for k in HALVES[h]:
+            if k > 0:
+                to_twin(k).start()
+                sent.append(lambda k=k: to_twin(k).wait_send())
     exchange(p0, 2, 2, 0, 4, start)
     sent.append(lambda: exchange(p0, 2, 2, 0, 4, leave))
     exchange(q0, 0, 5, 6, 1, start, 5)
     sent.append(lambda: exchange(q0, 0, 5, 6, 1, leave, 5))
-    mine = part[own_rows, :]
-    for k in range(1, GROUPS):
+    mine = part[rows_of(0), :]
+    for k in ORDER[::-1][1:]:
         to_twin(k).wait_recv()
         mine = mine + part_in[k - 1]
-    whole[own_rows, :] = mine
-    for k in FAR_FIRST:
+    whole[rows_of(0), :] = mine
+    for k in ORDER[:-1]:
         from_owner(k).start()
         sent.append(lambda k=k: from_owner(k).wait_send())
     harm[:, 0] = mine[:MODES]
-    for k in range(1, GROUPS):
-        from_owner(k).wait_recv()
-
-    high, low = split(whole[...])
-    grad = dot(enc[0], high) + (dot(enc[0], low) + dot(enc[1], high))
-    grad_out[...] = grad.reshape(MEMBERS, SLOTS, RADII)
-    start_all(back_mate(grad_out, grad_in, 2))
-    sent.append(lambda: all_of(grad_out, grad_in, 2).wait_send())
-    grad_in[0] = grad_out[0]
+
+    for h in (1, 0):
+        for k in HALVES[h]:
+            if k > 0:
+                from_owner(GROUPS - k).wait_recv()
+        high, low = split(whole[h * 128 : (h + 1) * 128])
+        grad = dot(enc[h, 0], high) + (dot(enc[h, 0], low) + dot(enc[h, 1], high))
+        grad_out[h] = grad.reshape(MEMBERS, PART, RADII)
+        start_all(back_mate(grad_out.at[h], grad_in.at[h], 3 + h))
+        sent.append(lambda h=h: all_of(grad_out.at[h], grad_in.at[h], 3 + h).wait_send())
+        grad_in[h, 0] = grad_out[h, 0]
     exchange(p0, 2, 2, 0, 4, arrive)
-    all_of(grad_out, grad_in, 2).wait_recv()
+    for h in (1, 0):
+        all_of(grad_out.at[h], grad_in.at[h], 3 + h).wait_recv()
     high, low = split(grad_in[...].reshape(ROWS, RADII) * factor[...])
     impulse = dot(pick_t[...], high) + dot(pick_t[...], low)
     impulse = impulse.reshape(PLANES, COLS, RADII)
@@ -813,22 +819,22 @@
             pltpu.VMEM((ROWS, 128), F32),
             pltpu.VMEM((MEMBERS, 8, LANES), F32),
             pltpu.VMEM((MEMBERS, 8, LANES), F32),
-            pltpu.VMEM((2, ROWS, LANES), BF16),
-            pltpu.VMEM((2, LANES, ROWS), BF16),
-            pltpu.VMEM((MEMBERS, SLOTS, RADII), F32),
-            pltpu.VMEM((MEMBERS, SLOTS, RADII), F32),
+            pltpu.VMEM((2, 2, MEMBERS * PART, 128), BF16),
+            pltpu.VMEM((2, 2, 128, MEMBERS * PART), BF16),
+            pltpu.VMEM((2, MEMBERS, PART, RADII), F32),
+            pltpu.VMEM((2, MEMBERS, PART, RADII), F32),
             pltpu.VMEM((GROUPS * WAVES, RADII), F32),
             pltpu.VMEM((GROUPS - 1, WAVES, RADII), F32),
             pltpu.VMEM((GROUPS * WAVES, RADII), F32),
-            pltpu.VMEM((MEMBERS, SLOTS, RADII), F32),
-            pltpu.VMEM((MEMBERS, SLOTS, RADII), F32),
+            pltpu.VMEM((2, MEMBERS, PART, RADII), F32),
+            pltpu.VMEM((2, MEMBERS, PART, RADII), F32),
             pltpu.SemaphoreType.DMA((11,)),
             pltpu.SemaphoreType.DMA((6, 4)),
             pltpu.SemaphoreType.DMA((6, 4)),
             pltpu.SemaphoreType.DMA((2, 9)),
             pltpu.SemaphoreType.DMA((2, 9)),
-            pltpu.SemaphoreType.DMA((3,)),
-            pltpu.SemaphoreType.DMA((3,)),
+            pltpu.SemaphoreType.DMA((5,)),
+            pltpu.SemaphoreType.DMA((5,)),
             pltpu.SemaphoreType.DMA((2, GROUPS - 1)),
             pltpu.SemaphoreType.DMA((2, GROUPS - 1)),
         ],

time: 77.3 us -> 75.1 us (0.972)
  Pallas kernels: 73.5 us -> 71.4 us
    pallas_call x1, Pallas kernels: 73.5 us -> 71.4 us  [local(): pl.pallas_call(kernel, out_shape=(jax.ShapeDtypeStruct((5, PLANES, COLS,...]
where the time goes in v4:
time: 75.1 us; the launch traced here: 75 us
  Pallas kernels  71.4 us (95%)
  local copies, waits for them, and re-layouts  2.33 us (3%)
  between operations  1.3 us (2%)
    pallas_call x1, Pallas kernels, local(): pl.pallas_call(kernel, out_shape=(jax.ShapeDtypeStruct((5, PLANES, COLS,...  71.4 us
    unnamed x4, local copies, waits for them, and re-layouts  2.33 us

profile of v4, /device:TPU:1, one launch (start us, length us, event | category | flops | bytes accessed | tf_op | source)
XLA Modules:
  0.0 75.0 jit_solution(1081466970891450395)
XLA Ops:
  1.3 71.4 %shard_map.122 = (f32[5,16,8,128]{3,2,1,0:T(8,128)}, f32[31,1,128]{2,1,0:T(1,128)}) custom-call(f32[5,16,8,128]{3,2,1,0:T(8,128)} %state.1, f32[16,8,128]{2,1,0:T(8,128)} %mean.1, f32[16,8,128]{2,1,0:T(8,128)} %sound.1, f32[5,5]{1,0:T(8,128)} %flux_a_in.1, f32[5,5]{1,0:T(8,128)} %flux_r_in.1, f32[5,5]{1,0:T(8,128)} %flux_t_in.1, s32[1,8]{1,0:T(1,128)} %pair_in.1, ...), custom_call_target="tpu_custom_call" | custom-call | tf_op jit(solution)/shard_map/pallas_call | solution.py:788
  72.6 0.0 copy-start
  72.7 1.7 %copy.17 = f32[5,16,8,128]{3,2,1,0:T(8,128)} copy(f32[5,16,8,128]{3,2,1,0:T(8,128)} %get-tuple-element.10) | data formatting | bytes 655360
  74.4 0.0 copy-done
  74.4 0.6 copy.18
Async XLA Ops:
  72.6 1.7 %copy-start = (f32[31,1,128]{2,1,0:T(1,128)S(1)}, f32[31,1,128]{2,1,0:T(1,128)}, u32[]{:S(2)}) copy-start(f32[31,1,128]{2,1,0:T(1,128)} %get-tuple-element.5) | copy-start | bytes 47620

commit v5 on v4

--- a/solution.py
+++ b/solution.py
@@ -33,7 +33,7 @@
 HALVES = (ORDER[: GROUPS // 2], ORDER[GROUPS // 2 :])
 PART = SLOTS // 2
 UNROLL = 4
-VMEM_GRANT = 60 << 20
+VMEM_GRANT = 32 << 20
 MESH = pl.DeviceIdType.MESH
 F32, BF16, I32 = jnp.float32, jnp.bfloat16, jnp.int32
 
@@ -842,16 +842,21 @@
             collective_id=0, has_side_effects=True, vmem_limit_bytes=VMEM_GRANT
         ),
     )(
-        state,
-        mean_velocity,
-        sound_speed,
-        flux_axial,
-        flux_radial,
-        flux_azimuthal,
-        axis_pair,
-        panel_weight,
-        panel_cell,
-        panel_owner.reshape(1, PANELS),
+        *(
+            pltpu.with_memory_space_constraint(argument, pltpu.HBM)
+            for argument in (
+                state,
+                mean_velocity,
+                sound_speed,
+                flux_axial,
+                flux_radial,
+                flux_azimuthal,
+                axis_pair,
+                panel_weight,
+                panel_cell,
+                panel_owner.reshape(1, PANELS),
+            )
+        ),
         panel_count,
     )
     return fields, rows.reshape(1, 1, MODES, RADII)

time: 75.1 us -> 73.4 us (0.977)
  local copies, waits for them, and re-layouts: 2.33 us -> 1.33 us
  Pallas kernels: 71.4 us -> 70.6 us
    unnamed x4 -> x2, local copies, waits for them, and re-layouts: 2.33 us -> 1.33 us
where the time goes in v5:
time: 73.4 us; the launch traced here: 73.2 us
  Pallas kernels  70.6 us (96%)
  local copies, waits for them, and re-layouts  1.33 us (2%)
  between operations  1.29 us (2%)
    pallas_call x1, Pallas kernels, local(): pl.pallas_call(kernel, out_shape=(jax.ShapeDtypeStruct((5, PLANES, COLS,...  70.6 us

profile of v5, /device:TPU:1, one launch (start us, length us, event | category | flops | bytes accessed | tf_op | source)
XLA Modules:
  0.0 73.2 jit_solution(10527734870526960528)
XLA Ops:
  1.3 70.6 %shard_map.122 = (f32[5,16,8,128]{3,2,1,0:T(8,128)S(1)}, f32[31,1,128]{2,1,0:T(1,128)S(1)}) custom-call(f32[5,16,8,128]{3,2,1,0:T(8,128)} %state.1, f32[16,8,128]{2,1,0:T(8,128)} %mean.1, f32[16,8,128]{2,1,0:T(8,128)} %sound.1, f32[5,5]{1,0:T(8,128)} %flux_a_in.1, f32[5,5]{1,0:T(8,128)} %flux_r_in.1, f32[5,5]{1,0:T(8,128)} %flux_t_in.1, s32[1,8]{1,0:T(1,128)} %pair_in.1, ...), custom_call_target="tpu_custom_call" | custom-call | tf_op jit(solution)/shard_map/pallas_call | solution.py:788
  71.9 0.7 copy.17
  72.6 0.6 copy.18

commit v6 on v5

--- a/solution.py
+++ b/solution.py
@@ -32,7 +32,7 @@
 ORDER = (4, 3, 5, 2, 6, 1, 7, 0)
 HALVES = (ORDER[: GROUPS // 2], ORDER[GROUPS // 2 :])
 PART = SLOTS // 2
-UNROLL = 4
+UNROLL = 8
 VMEM_GRANT = 32 << 20
 MESH = pl.DeviceIdType.MESH
 F32, BF16, I32 = jnp.float32, jnp.bfloat16, jnp.int32
@@ -469,7 +469,7 @@
                 ref[f, i + skip] += jnp.where(ray == 0, zero, jnp.where(ray == 1, one, 0.0))
             return carry
 
-        lax.fori_loop(0, PLANES, step, 0, unroll=4)
+        lax.fori_loop(0, PLANES, step, 0, unroll=PLANES)
 
     def beside(value, level, f, i):
         before = jnp.broadcast_to(col_recv[level, 1, pl.ds(f * PLANES + i, 1), :], (8, 128))

time: 73.4 us -> 74.5 us (1.015)
  Pallas kernels: 70.6 us -> 71.7 us
    pallas_call x1, Pallas kernels: 70.6 us -> 71.7 us  [local(): pl.pallas_call(kernel, out_shape=(jax.ShapeDtypeStruct((5, PLANES, COLS,...]
where the time goes in v6:
time: 74.5 us; the launch traced here: 74.3 us
  Pallas kernels  71.7 us (96%)
  local copies, waits for them, and re-layouts  1.33 us (2%)
  between operations  1.29 us (2%)
    pallas_call x1, Pallas kernels, local(): pl.pallas_call(kernel, out_shape=(jax.ShapeDtypeStruct((5, PLANES, COLS,...  71.7 us

profile of v6, /device:TPU:1, one launch (start us, length us, event | category | flops | bytes accessed | tf_op | source)
XLA Modules:
  0.0 74.3 jit_solution(11401482855029341716)
XLA Ops:
  1.3 71.7 %shard_map.122 = (f32[5,16,8,128]{3,2,1,0:T(8,128)S(1)}, f32[31,1,128]{2,1,0:T(1,128)S(1)}) custom-call(f32[5,16,8,128]{3,2,1,0:T(8,128)} %state.1, f32[16,8,128]{2,1,0:T(8,128)} %mean.1, f32[16,8,128]{2,1,0:T(8,128)} %sound.1, f32[5,5]{1,0:T(8,128)} %flux_a_in.1, f32[5,5]{1,0:T(8,128)} %flux_r_in.1, f32[5,5]{1,0:T(8,128)} %flux_t_in.1, s32[1,8]{1,0:T(1,128)} %pair_in.1, ...), custom_call_target="tpu_custom_call" | custom-call | tf_op jit(solution)/shard_map/pallas_call | solution.py:788
  73.0 0.7 copy.17
  73.7 0.6 copy.18
